TPU v7x, 32 devices: a whole 2x2x4 slice. The times are simulated.
32 devices in a mesh: dp: 4 (over y, x), seq: 8 (over z, core).
Axes of the slice: x: 2, y: 2, z: 4, core: 2. Of those that a mesh axis runs over, the one named last changes fastest.
Arguments:
- features: bfloat16 [6144, 1408], P(('dp', 'seq')), parts along dimension 0, may hold values from -6 to 6
- norm_gain: float32 [1408], replicated, may hold values from 0.1 to 1.9
- conv_weight: bfloat16 [5, 1408, 1536], P(None, None, 'seq'), may hold values from -0.0625 to 0.0625
- conv_bias: float32 [1536], replicated, may hold values from -3 to 3
- attn_gain: float32 [1536], replicated, may hold values from 0.1 to 1.9
- query_weight: bfloat16 [1536, 1024], P('seq'), may hold values from -1 to 1
- keyval_weight: bfloat16 [1536, 256], P('seq'), may hold values from -1 to 1
- head_scale: float32 [8], replicated, may hold values from 1 to 4
- output_weight: bfloat16 [1024, 1536], P('seq'), may hold values from -0.1875 to 0.1875
Outputs:
- coarse: bfloat16 [3072, 1536], P(('dp', 'seq')), parts along dimension 0
- attended: bfloat16 [3072, 1536], P(('dp', 'seq')), parts along dimension 0
There are 4 independent parts, one for each index of `dp`. A program takes and returns all parts, laid end to end along the dimension named above; an argument that names none is the same for every part. Nothing has to cross between parts.
All inputs are finite; a program needn't handle non-finite values.
Results may differ from a plain program's by a relative error of at most 0.007.
Values may be sent and summed in bfloat16 or wider, within the bound.
A program may use at most 128 MiB of HBM per device.

v0:
```python
import jax
import jax.numpy as jnp
from jax import lax
from jax.sharding import PartitionSpec as P

HEAD_DIM = 128


def with_halo(block, sides, width):
    for axis, dim in sides:
        count = lax.axis_size(axis)
        forward = [(i, i + 1) for i in range(count - 1)]
        backward = [(target, source) for source, target in forward]
        low = lax.ppermute(
            lax.slice_in_dim(block, block.shape[dim] - width, None, axis=dim), axis, forward
        )
        high = lax.ppermute(lax.slice_in_dim(block, 0, width, axis=dim), axis, backward)
        block = jnp.concatenate([low, block, high], axis=dim)
    return block


def normalize(values_in, channel_gain):
    meansq = jnp.mean(values_in * values_in, axis=-1, keepdims=True)
    return values_in * lax.rsqrt(meansq + 1e-06) * channel_gain


def convolve(padded, kernel, row_count):
    summed = jnp.zeros((row_count, kernel.shape[2]), jnp.float32)
    for kernel_tap in range(kernel.shape[0]):
        summed = summed + jnp.dot(
            padded[kernel_tap : kernel_tap + row_count],
            kernel[kernel_tap],
            preferred_element_type=jnp.float32,
        )
    return summed


def pool_pairs(levels):
    return jnp.max(levels.reshape(-1, 2, levels.shape[1]), axis=1)


def attend(queries, keyvals, scales):
    row_count = queries.shape[0]
    head_count = scales.shape[0]
    shaped = queries.reshape(row_count, head_count, HEAD_DIM)
    key_block = lax.all_gather(keyvals, "seq", axis=0, tiled=True)
    running_max = jnp.full((head_count, row_count), -1e30, jnp.float32)
    key_part = key_block[:, :HEAD_DIM]
    value_part = key_block[:, HEAD_DIM:]
    scores = (
        jnp.einsum("qhd,kd->hqk", shaped, key_part, preferred_element_type=jnp.float32)
        * scales[:, None, None]
        * HEAD_DIM ** (-0.5)
    )
    newest = jnp.maximum(running_max, jnp.max(scores, axis=2))
    expon = jnp.exp(scores - newest[:, :, None])
    running_sum = jnp.sum(expon, axis=2)
    running_ctx = jnp.einsum(
        "hqk,kd->hqd", expon.astype(jnp.bfloat16), value_part, preferred_element_type=jnp.float32
    )
    context = running_ctx / running_sum[:, :, None]
    return context.transpose(1, 0, 2).reshape(row_count, head_count * HEAD_DIM).astype(jnp.bfloat16)


def shards(
    features,
    norm_gain,
    conv_weight,
    conv_bias,
    attn_gain,
    query_weight,
    keyval_weight,
    head_scale,
    output_weight,
):
    normed = jax.nn.gelu(normalize(features.astype(jnp.float32), norm_gain)).astype(jnp.bfloat16)
    fine_rows = normed.shape[0]
    padded = with_halo(normed, (("seq", 0),), 2)
    levels = (
        convolve(padded, lax.all_gather(conv_weight, "seq", axis=2, tiled=True), fine_rows)
        + conv_bias[None, :]
    )
    coarse = pool_pairs(levels).astype(jnp.bfloat16)
    attn_in = normalize(coarse.astype(jnp.float32), attn_gain).astype(jnp.bfloat16)
    columns = attn_in
    query_sum = jnp.dot(
        columns,
        lax.all_gather(query_weight, "seq", axis=0, tiled=True),
        preferred_element_type=jnp.float32,
    )
    keyval_sum = jnp.dot(
        columns,
        lax.all_gather(keyval_weight, "seq", axis=0, tiled=True),
        preferred_element_type=jnp.float32,
    )
    queries = query_sum.astype(jnp.bfloat16)
    keyvals = keyval_sum.astype(jnp.bfloat16)
    context = attend(queries, keyvals, head_scale)
    columns = context
    projected = jnp.dot(
        columns,
        lax.all_gather(output_weight, "seq", axis=0, tiled=True),
        preferred_element_type=jnp.float32,
    )
    return (coarse, projected.astype(jnp.bfloat16))


def solution(mesh):
    return jax.shard_map(
        shards,
        mesh=mesh,
        in_specs=(
            P(("dp", "seq"), None),
            P(),
            P(None, None, "seq"),
            P(),
            P(),
            P("seq", None),
            P("seq", None),
            P(),
            P("seq", None),
        ),
        out_specs=(P(("dp", "seq"), None), P(("dp", "seq"), None)),
        check_vma=False,
    )
```

profile of v0, /device:TPU:1, one launch (start us, length us, event | category | flops | bytes accessed | tf_op | source)
XLA Modules:
  0.0 296.6 jit_solution(16891048494871343277)
XLA Ops:
  7.2 0.0 copy-start.1
  7.2 0.0 copy-start.3
  7.2 0.0 copy-start.2
  7.2 0.0 all-gather.4.cloned.1.call-start
  7.2 0.7 all-gather.4.cloned.1.call-update
  7.9 0.0 all-gather.6.cloned.1.call-start
  8.0 0.7 all-gather.6.cloned.1.call-update
  8.7 0.0 all-gather.8.cloned.1.call-start
  8.7 0.7 all-gather.8.cloned.1.call-update
  9.4 0.0 copy-done.1
  9.4 0.2 fusion.24
  9.6 0.0 copy-done.3
  9.6 0.5 fusion.28
  10.2 2.0 collective-permute-start.1
  12.1 4.5 %collective-permute-start = (bf16[2,1408]{1,0:T(2,128)(2,1)S(1)}, bf16[2,1408]{1,0:T(2,128)(2,1)S(1)}, u32[]{:S(2)}, u32[]{:S(2)}) collective-permute-start(bf16[2,1408]{1,0:T(2,128)(2,1)S(1)} %get-tuple-element.2), channel_id=1, source_target_pairs={{0,1},{1,2},{2,3},{3,4},{4,5},{5,6},{6,7},{8,9},{9,10},{10,11},{11... | collective-permute-start | bytes 16904 | tf_op jit(solution)/shard_map/ppermute | solution.py:14
  16.7 0.0 copy-done.2
  16.7 18.2 %all_gather.16 = bf16[1536,256]{1,0:T(8,128)(2,1)S(1)} all-gather(bf16[192,256]{1,0:T(8,128)(2,1)S(1)} %copy-done.2), channel_id=1, replica_groups=mesh['dp'=4,'seq'=8] {'seq'}, dimensions={0}, use_global_device_ids=true | all-gather | bytes 884736 | tf_op jit(solution)/shard_map/all_gather | solution.py:93
  35.0 0.0 collective-permute-done
  35.0 170.4 %all-gather.4.cloned.1.call-done = bf16[5,1408,1536]{1,2,0:T(8,128)(2,1)} async-done(((bf16[5,1408,192]{1,2,0:T(8,128)(2,1)}), bf16[5,1408,1536]{1,2,0:T(8,128)(2,1)}) %all-gather.4.cloned.1.call-update) | async-done | bytes 21626896 | tf_op jit(solution)/shard_map/all_gather | solution.py:80
  205.4 3.8 %fusion.3 = f32[192,1536]{1,0:T(8,128)S(1)} fusion(bf16[5,1408,1536]{1,2,0:T(8,128)(2,1)} %all-gather.4.cloned.1.call-done, bf16[192,1408]{1,0:T(8,128)(2,1)S(1)} %fusion.28, bf16[2,1408]{1,0:T(2,128)(2,1)S(1)} %collective-permute-done), kind=kOutput, calls=%fused_computation.7 | convolution fusion | flops 831553536 | bytes 6051328 | tf_op jit(solution)/shard_map/dot_general | solution.py:30
  209.2 0.0 collective-permute-done.1
  209.2 3.8 %fusion = f32[192,1536]{1,0:T(8,128)S(1)} fusion(bf16[5,1408,1536]{1,2,0:T(8,128)(2,1)} %all-gather.4.cloned.1.call-done, bf16[2,1408]{1,0:T(2,128)(2,1)S(1)} %collective-permute-done.1, bf16[192,1408]{1,0:T(8,128)(2,1)S(1)} %fusion.28), kind=kOutput, calls=%fused_computation.1 | convolution fusion | flops 831553536 | bytes 6051328 | tf_op jit(solution)/shard_map/dot_general | solution.py:30
  213.0 4.2 %fusion.2 = f32[192,1536]{1,0:T(8,128)S(1)} fusion(bf16[192,1408]{1,0:T(8,128)(2,1)S(1)} %fusion.28, bf16[5,1408,1536]{1,2,0:T(8,128)(2,1)} %all-gather.4.cloned.1.call-done), kind=kOutput, calls=%fused_computation.5 | convolution fusion | flops 830472192 | bytes 6045696 | tf_op jit(solution)/shard_map/dot_general | solution.py:30
  217.2 0.0 copy-start.5
  217.2 3.8 %fusion.1 = f32[192,1536]{1,0:T(8,128)S(1)} fusion(bf16[5,1408,1536]{1,2,0:T(8,128)(2,1)} %all-gather.4.cloned.1.call-done, bf16[192,1408]{1,0:T(8,128)(2,1)S(1)} %fusion.28, bf16[2,1408]{1,0:T(2,128)(2,1)S(1)} %collective-permute-done.1), kind=kOutput, calls=%fused_computation.3 | convolution fusion | flops 831553536 | bytes 6051328 | tf_op jit(solution)/shard_map/dot_general | solution.py:30
  221.1 0.0 copy-done.5
  221.1 4.0 %fusion.9 = bf16[192,1536]{1,0:T(8,128)(2,1)S(1)} fusion(f32[192,1536]{1,0:T(8,128)S(1)} %fusion, f32[192,1536]{1,0:T(8,128)S(1)} %fusion.1, f32[192,1536]{1,0:T(8,128)S(1)} %fusion.2, f32[192,1536]{1,0:T(8,128)S(1)} %fusion.3, bf16[5,1408,1536]{1,2,0:T(8,128)(2,1)} %all-gather.4.cloned.1.call-done, f32[1536]{0:T(1024)S(1)} %copy-done.5, ...), kind=kOutput, calls=%fused_computation.14 | convolution fusion | flops 833323008 | bytes 10186240 | tf_op jit(solution)/shard_map/dot_general | solution.py:30
  225.0 0.0 copy-start.4
  225.1 0.2 reshape.36
  225.3 1.6 reduce_max.18
  226.9 0.0 copy-start
  226.9 0.2 fusion.34
  227.1 0.0 copy-done.4
  227.1 0.0 copy-start.6
  227.1 0.3 convolution_convert_fusion.2
  227.4 16.3 %all_gather.17 = bf16[768,256]{1,0:T(8,128)(2,1)S(1)} all-gather(bf16[96,256]{1,0:T(8,128)(2,1)S(1)} %convolution_convert_fusion.2), channel_id=1, replica_groups=mesh['dp'=4,'seq'=8] {'seq'}, dimensions={0}, use_global_device_ids=true | all-gather | bytes 442368 | tf_op jit(solution)/shard_map/all_gather | solution.py:46
  243.7 4.3 %all-gather.6.cloned.1.call-done = bf16[1536,1024]{1,0:T(8,128)(2,1)} async-done(((bf16[192,1024]{1,0:T(8,128)(2,1)}), bf16[1536,1024]{1,0:T(8,128)(2,1)}) %all-gather.6.cloned.1.call-update) | async-done | bytes 3145744 | tf_op jit(solution)/shard_map/all_gather | solution.py:88
  248.0 2.6 fusion.20
  250.6 0.0 copy-done
  250.6 0.0 copy-done.6
  250.6 0.6 bitcast_reduce_fusion
  251.2 0.7 fusion.11
  251.8 0.7 fusion.21
  252.6 34.2 %all-gather.8.cloned.1.call-done = bf16[1024,1536]{1,0:T(8,128)(2,1)} async-done(((bf16[128,1536]{1,0:T(8,128)(2,1)}), bf16[1024,1536]{1,0:T(8,128)(2,1)}) %all-gather.8.cloned.1.call-update) | async-done | bytes 3145744 | tf_op jit(solution)/shard_map/all_gather | solution.py:102
  286.8 3.2 %convolution_convert_fusion = bf16[96,1536]{1,0:T(8,128)(2,1)} fusion(bf16[1024,1536]{1,0:T(8,128)(2,1)} %all-gather.8.cloned.1.call-done, bf16[8,12,8,128]{3,2,1,0:T(8,128)(2,1)S(1)} %fusion.21), kind=kOutput, calls=%fused_computation.19 | convolution fusion | flops 302137344 | bytes 3637248 | tf_op jit(solution)/shard_map/dot_general | solution.py:100
  (4 shorter events, 0.0 us)
Async XLA Ops:
  7.2 2.3 copy-start.1
  7.2 2.4 copy-start.3
  7.2 9.5 %copy-start.2 = (bf16[192,256]{1,0:T(8,128)(2,1)S(1)}, bf16[192,256]{1,0:T(8,128)(2,1)}, u32[]{:S(2)}) copy-start(bf16[192,256]{1,0:T(8,128)(2,1)} %param.15) | copy-start | bytes 294916
  7.2 198.2 %all-gather.4.cloned.1.call-start = ((), (), s32[]{:S(2)}) async-start(), calls=%async_computation | async-start | bytes 24330240 | tf_op jit(solution)/shard_map/all_gather | solution.py:80
  7.9 240.1 %all-gather.6.cloned.1.call-start = ((), (), s32[]{:S(2)}) async-start(), calls=%async_computation.1 | async-start | bytes 3538944 | tf_op jit(solution)/shard_map/all_gather | solution.py:88
  8.7 278.1 %all-gather.8.cloned.1.call-start = ((), (), s32[]{:S(2)}) async-start(), calls=%async_computation.2 | async-start | bytes 3538944 | tf_op jit(solution)/shard_map/all_gather | solution.py:102
  10.2 199.0 %collective-permute-start.1 = (bf16[2,1408]{1,0:T(2,128)(2,1)S(1)}, bf16[2,1408]{1,0:T(2,128)(2,1)S(1)}, u32[]{:S(2)}, u32[]{:S(2)}) collective-permute-start(bf16[2,1408]{1,0:T(2,128)(2,1)S(1)} %get-tuple-element.3), channel_id=1, source_target_pairs={{1,0},{2,1},{3,2},{4,3},{5,4},{6,5},{7,6},{9,8},{10,9},{11,10},{12... | collective-permute-start | bytes 16904 | tf_op jit(solution)/shard_map/ppermute | solution.py:17
  12.1 22.8 %collective-permute-start = (bf16[2,1408]{1,0:T(2,128)(2,1)S(1)}, bf16[2,1408]{1,0:T(2,128)(2,1)S(1)}, u32[]{:S(2)}, u32[]{:S(2)}) collective-permute-start(bf16[2,1408]{1,0:T(2,128)(2,1)S(1)} %get-tuple-element.2), channel_id=1, source_target_pairs={{0,1},{1,2},{2,3},{3,4},{4,5},{5,6},{6,7},{8,9},{9,10},{10,11},{11... | collective-permute-start | bytes 16904 | tf_op jit(solution)/shard_map/ppermute | solution.py:14
  217.2 3.9 %copy-start.5 = (f32[1536]{0:T(1024)S(1)}, f32[1536]{0:T(1024)}, u32[]{:S(2)}) copy-start(f32[1536]{0:T(1024)} %param.12) | copy-start | bytes 18436
  225.0 2.0 copy-start.4
  226.9 23.7 %copy-start = (bf16[96,1536]{1,0:T(8,128)(2,1)}, bf16[96,1536]{1,0:T(8,128)(2,1)S(1)}, u32[]{:S(2)}) copy-start(bf16[96,1536]{1,0:T(8,128)(2,1)S(1)} %reduce_max.18) | copy-start | bytes 884740
  227.1 23.5 %copy-start.6 = (f32[8]{0:T(128)S(1)}, f32[8]{0:T(128)}, u32[]{:S(2)}) copy-start(f32[8]{0:T(128)} %param.16) | copy-start | bytes 100
Sparse Core Ops, SparseCore 0:
  9.6 195.6 all-gather.3
  207.0 40.9 all-gather.5
  249.6 37.1 all-gather.7
where the time goes:
time: 297 us
  waiting for transfers between devices  211 us (71%)
  blocking collectives  34.5 us (12%)
  matrix products  27 us (9%)
  between operations  14 us (5%)
  starting transfers between devices  6.63 us (2%)
  other arithmetic  3.16 us (1%)
    all_gather x1, waiting for transfers between devices, shards(): lax.all_gather(conv_weight, 'seq', axis=2, tiled=True)  170 us
    all_gather x1, waiting for transfers between devices, shards(): lax.all_gather(output_weight, 'seq', axis=0, tiled=True)  34.2 us
    dot_general x5, matrix products, convolve(): jnp.dot(padded[kernel_tap:kernel_tap + row_count], kernel[kernel_tap], pr...  19.6 us
    all_gather x1, blocking collectives, shards(): lax.all_gather(keyval_weight, 'seq', axis=0, tiled=True)  18.2 us
    all_gather x1, blocking collectives, attend(): key_block = lax.all_gather(keyvals, 'seq', axis=0, tiled=True)  16.3 us
  transfers between devices with their start and end apart: 5, of which 3 were waited for; matrix products, arithmetic and copies ran while one was open for 9% of the time, Pallas kernels for 0%

commit v1 on v0

--- a/solution.py
+++ b/solution.py
@@ -74,13 +74,15 @@
     output_weight,
 ):
     normed = jax.nn.gelu(normalize(features.astype(jnp.float32), norm_gain)).astype(jnp.bfloat16)
-    fine_rows = normed.shape[0]
-    padded = with_halo(normed, (("seq", 0),), 2)
-    levels = (
-        convolve(padded, lax.all_gather(conv_weight, "seq", axis=2, tiled=True), fine_rows)
-        + conv_bias[None, :]
-    )
-    coarse = pool_pairs(levels).astype(jnp.bfloat16)
+    window = lax.all_gather(normed, "seq", axis=0, tiled=True)
+    fine_rows = window.shape[0]
+    width = conv_weight.shape[0] // 2
+    padded = jnp.pad(window, ((width, width), (0, 0)))
+    channels = conv_weight.shape[2]
+    own_bias = lax.dynamic_slice_in_dim(conv_bias, lax.axis_index("seq") * channels, channels)
+    levels = convolve(padded, conv_weight, fine_rows) + own_bias[None, :]
+    pooled = pool_pairs(levels).astype(jnp.bfloat16)
+    coarse = lax.all_to_all(pooled, "seq", split_axis=0, concat_axis=1, tiled=True)
     attn_in = normalize(coarse.astype(jnp.float32), attn_gain).astype(jnp.bfloat16)
     columns = attn_in
     query_sum = jnp.dot(

time: 297 us -> 165 us (0.56)
  waiting for transfers between devices: 211 us -> 67.8 us
  blocking collectives: 34.5 us -> 50.8 us
  matrix products: 27 us -> 17.9 us
  other arithmetic: 3.16 us -> 7 us
    all_gather x1, waiting for transfers between devices: 170 us -> 48.8 us  [shards(): window = lax.all_gather(normed, 'seq', axis=0, tiled=True)]
    all_gather x1, waiting for transfers between devices: 34.2 us -> 17.6 us  [shards(): lax.all_gather(output_weight, 'seq', axis=0, tiled=True)]
    all_gather x1, blocking collectives: 18.2 us -> 34.8 us  [shards(): lax.all_gather(keyval_weight, 'seq', axis=0, tiled=True)]
    dot_general x5, matrix products: 19.6 us -> 10.4 us  [convolve(): jnp.dot(padded[kernel_tap:kernel_tap + row_count], kernel[kernel_tap], pr...]
    ppermute x2 -> x0, starting transfers between devices: 6.52 us -> none  [the longest x1 4.55 us: with_halo(): lax.ppermute(lax.slice_in_dim(block, block.shape[dim] - width, None, axis...]
    all_gather x1, waiting for transfers between devices: 4.31 us -> 0.01 us  [shards(): lax.all_gather(query_weight, 'seq', axis=0, tiled=True)]
    all_to_all x0 -> x1, starting transfers between devices: none -> 3.64 us  [shards(): lax.all_to_all(pooled, 'seq', split_axis=0, concat_axis=1, tiled=True)]
  transfers between devices with their start and end apart: 5 -> 4, of which waited for: 3 -> 2; matrix products, arithmetic and copies ran while one was open for 9% -> 13% of each run, Pallas kernels for 0% -> 0%
where the time goes in v1:
time: 165 us; the launch traced here: 164 us
  waiting for transfers between devices  67.8 us (41%)
  blocking collectives  50.8 us (31%)
  matrix products  17.9 us (11%)
  between operations  13.9 us (8%)
  other arithmetic  7 us (4%)
  starting transfers between devices  3.76 us (2%)
  local copies, waits for them, and re-layouts  3.07 us (2%)
    all_gather x1, waiting for transfers between devices, shards(): window = lax.all_gather(normed, 'seq', axis=0, tiled=True)  48.8 us
    all_gather x1, blocking collectives, shards(): lax.all_gather(keyval_weight, 'seq', axis=0, tiled=True)  34.8 us
    all_gather x1, waiting for transfers between devices, shards(): lax.all_gather(output_weight, 'seq', axis=0, tiled=True)  17.6 us
    all_gather x1, blocking collectives, attend(): key_block = lax.all_gather(keyvals, 'seq', axis=0, tiled=True)  16 us
    dot_general x5, matrix products, convolve(): jnp.dot(padded[kernel_tap:kernel_tap + row_count], kernel[kernel_tap], pr...  10.4 us
    all_to_all x1, starting transfers between devices, shards(): lax.all_to_all(pooled, 'seq', split_axis=0, concat_axis=1, tiled=True)  3.64 us
  transfers between devices with their start and end apart: 4, of which 2 were waited for; matrix products, arithmetic and copies ran while one was open for 13% of the time, Pallas kernels for 0%

profile of v1, /device:TPU:1, one launch (start us, length us, event | category | flops | bytes accessed | tf_op | source)
XLA Modules:
  0.0 164.2 jit_solution(5584520462857300883)
XLA Ops:
  7.2 0.0 copy-start.5
  7.2 0.0 all-gather.4.cloned.1.call-start
  7.2 1.4 fusion.41
  8.6 2.4 %fusion.45 = bf16[192,1408]{1,0:T(8,128)(2,1)} fusion(bf16[192,1408]{1,0:T(8,128)(2,1)} %param.9, f32[1408]{0:T(1024)} %param.10, f32[192]{0:T(256)S(1)} %add_rsqrt_fusion), kind=kLoop, calls=%fused_computation.40 | loop fusion | flops 3244032 | bytes 1087744 | tf_op jit(solution)/shard_map/convert_element_type | solution.py:76
  11.0 0.0 all-gather.4.cloned.1.call-update
  11.0 0.0 all-gather.6.cloned.1.call-start
  11.1 0.7 all-gather.6.cloned.1.call-update
  11.8 0.0 all-gather.8.cloned.1.call-start
  11.8 0.7 all-gather.8.cloned.1.call-update
  12.5 0.8 dynamic_slice.3
  13.3 48.8 %all-gather.4.cloned.1.call-done = bf16[1536,1408]{1,0:T(8,128)(2,1)} async-done(((bf16[192,1408]{1,0:T(8,128)(2,1)}), bf16[1536,1408]{1,0:T(8,128)(2,1)}) %all-gather.4.cloned.1.call-update) | async-done | bytes 4325392 | tf_op jit(solution)/shard_map/all_gather | solution.py:77
  62.1 0.0 copy-done.5
  62.1 0.0 copy-start.4
  62.1 4.0 %fusion.2 = f32[1536,192]{0,1:T(8,128)S(1)} fusion(bf16[1536,1408]{1,0:T(8,128)(2,1)} %all-gather.4.cloned.1.call-done, bf16[5,1408,192]{1,2,0:T(8,128)(2,1)S(1)} %copy-done.5), kind=kOutput, calls=%fused_computation.2 | convolution fusion | flops 830472192 | bytes 6045696 | tf_op jit(solution)/shard_map/dot_general | solution.py:30
  66.1 0.0 copy-done.4
  66.1 1.6 fusion.4
  67.8 1.6 fusion.53
  69.3 1.7 %fusion.18 = f32[1536,192]{0,1:T(8,128)S(1)} fusion(f32[1536,192]{0,1:T(8,128)S(1)} %fusion.2, f32[1536,192]{0,1:T(8,128)S(1)} %fusion.53, f32[1536,192]{0,1:T(8,128)S(1)} %fusion.4, bf16[1536,1408]{1,0:T(8,128)(2,1)S(1)} %copy-done.4, bf16[5,1408,192]{1,2,0:T(8,128)(2,1)S(1)} %copy-done.5), kind=kOutput, calls=%fused_computation.14 | convolution fusion | flops 831356928 | bytes 9584640 | tf_op jit(solution)/shard_map/dot_general | solution.py:30
  71.0 1.6 fusion.24
  72.6 0.3 copy.25
  72.9 0.4 reshape.41
  73.3 0.0 copy-start.1
  73.3 2.3 %reduce_max.18 = bf16[768,192]{1,0:T(8,128)(2,1)S(1)} reduce(bf16[768,2,192]{2,1,0:T(2,128)(2,1)S(1)} %reshape.41, bf16[]{:T(256)} %constant.84), dimensions={1}, to_apply=%region_1.2 | reduce | flops 147456 | bytes 884738 | tf_op jit(solution)/shard_map/reduce_max | solution.py:39
  75.6 0.0 copy-start.2
  75.6 0.2 copy.26
  75.8 0.4 convert_element_type.45
  76.2 0.8 copy.27
  77.1 3.6 %all-to-all-start = ((bf16[8,96,192]{1,2,0:T(8,128)(2,1)}), bf16[8,96,192]{1,2,0:T(8,128)(2,1)S(1)}, u32[]{:S(2)}, u32[]{:S(2)}) async-start(bf16[8,96,192]{1,2,0:T(8,128)(2,1)} %copy.27), calls=%async_computation | async-start | bytes 786432 | tf_op jit(solution)/shard_map/all_to_all | solution.py:85
  80.7 0.0 copy-done.1
  80.7 34.8 %all_gather.16 = bf16[1536,256]{1,0:T(8,128)(2,1)S(1)} all-gather(bf16[192,256]{1,0:T(8,128)(2,1)S(1)} %copy-done.1), channel_id=1, replica_groups=mesh['dp'=4,'seq'=8] {'seq'}, dimensions={0}, use_global_device_ids=true | all-gather | bytes 884736 | tf_op jit(solution)/shard_map/all_gather | solution.py:95
  115.5 0.0 all-to-all-done
  115.5 0.2 copy.31
  115.6 0.0 copy-start
  115.7 0.2 multiply_reduce_fusion
  115.9 0.0 copy-done.2
  115.9 0.0 copy-start.3
  115.9 0.3 convolution_convert_fusion.2
  116.2 16.0 %all_gather.17 = bf16[768,256]{1,0:T(8,128)(2,1)S(1)} all-gather(bf16[96,256]{1,0:T(8,128)(2,1)S(1)} %convolution_convert_fusion.2), channel_id=1, replica_groups=mesh['dp'=4,'seq'=8] {'seq'}, dimensions={0}, use_global_device_ids=true | all-gather | bytes 442368 | tf_op jit(solution)/shard_map/all_gather | solution.py:46
  132.2 0.0 all-gather.6.cloned.1.call-done
  132.2 2.6 %fusion.37 = bf16[12,8,8,128]{3,2,1,0:T(8,128)(2,1)S(1)} fusion(bf16[1536,1024]{1,0:T(8,128)(2,1)} %all-gather.6.cloned.1.call-done, bf16[96,1536]{1,0:T(8,128)(2,1)S(1)} %copy.31, f32[1536]{0:T(1024)S(1)} %copy-done.2, f32[96]{0:T(128)S(1)} %add_rsqrt_fusion.1), kind=kOutput, calls=%fused_computation.33 | convolution fusion | flops 302678016 | bytes 3643776 | tf_op jit(solution)/shard_map/dot_general | solution.py:88
  134.8 0.0 copy-done
  134.8 0.0 copy-done.3
  134.8 0.6 bitcast_reduce_fusion
  135.4 0.7 fusion.28
  136.1 0.7 fusion.38
  136.8 17.6 %all-gather.8.cloned.1.call-done = bf16[1024,1536]{1,0:T(8,128)(2,1)} async-done(((bf16[128,1536]{1,0:T(8,128)(2,1)}), bf16[1024,1536]{1,0:T(8,128)(2,1)}) %all-gather.8.cloned.1.call-update) | async-done | bytes 3145744 | tf_op jit(solution)/shard_map/all_gather | solution.py:104
  154.4 3.3 %convolution_convert_fusion = bf16[96,1536]{1,0:T(8,128)(2,1)} fusion(bf16[1024,1536]{1,0:T(8,128)(2,1)} %all-gather.8.cloned.1.call-done, bf16[8,12,8,128]{3,2,1,0:T(8,128)(2,1)S(1)} %fusion.38), kind=kOutput, calls=%fused_computation.21 | convolution fusion | flops 302137344 | bytes 3637248 | tf_op jit(solution)/shard_map/dot_general | solution.py:102
  (3 shorter events, 0.0 us)
Async XLA Ops:
  7.2 55.0 %copy-start.5 = (bf16[5,1408,192]{1,2,0:T(8,128)(2,1)S(1)}, bf16[5,1408,192]{1,2,0:T(8,128)(2,1)}, u32[]{:S(2)}) copy-start(bf16[5,1408,192]{1,2,0:T(8,128)(2,1)} %param.11) | copy-start | bytes 8110084
  7.2 55.0 %all-gather.4.cloned.1.call-start = ((), (), s32[]{:S(2)}) async-start(), calls=%async_computation.1 | async-start | bytes 4866048 | tf_op jit(solution)/shard_map/all_gather | solution.py:77
  11.0 121.2 %all-gather.6.cloned.1.call-start = ((), (), s32[]{:S(2)}) async-start(), calls=%async_computation.2 | async-start | bytes 3538944 | tf_op jit(solution)/shard_map/all_gather | solution.py:90
  11.8 142.6 %all-gather.8.cloned.1.call-start = ((), (), s32[]{:S(2)}) async-start(), calls=%async_computation.3 | async-start | bytes 3538944 | tf_op jit(solution)/shard_map/all_gather | solution.py:104
  62.1 4.0 %copy-start.4 = (bf16[1536,1408]{1,0:T(8,128)(2,1)S(1)}, bf16[1536,1408]{1,0:T(8,128)(2,1)}, u32[]{:S(2)}) copy-start(bf16[1536,1408]{1,0:T(8,128)(2,1)} %all-gather.4.cloned.1.call-done) | copy-start | bytes 12976132
  73.3 7.4 %copy-start.1 = (bf16[192,256]{1,0:T(8,128)(2,1)S(1)}, bf16[192,256]{1,0:T(8,128)(2,1)}, u32[]{:S(2)}) copy-start(bf16[192,256]{1,0:T(8,128)(2,1)} %param.15) | copy-start | bytes 294916
  75.6 40.3 %copy-start.2 = (f32[1536]{0:T(1024)S(1)}, f32[1536]{0:T(1024)}, u32[]{:S(2)}) copy-start(f32[1536]{0:T(1024)} %param.13) | copy-start | bytes 18436
  77.1 38.4 %all-to-all-start = ((bf16[8,96,192]{1,2,0:T(8,128)(2,1)}), bf16[8,96,192]{1,2,0:T(8,128)(2,1)S(1)}, u32[]{:S(2)}, u32[]{:S(2)}) async-start(bf16[8,96,192]{1,2,0:T(8,128)(2,1)} %copy.27), calls=%async_computation | async-start | bytes 786432 | tf_op jit(solution)/shard_map/all_to_all | solution.py:85
  115.6 19.2 %copy-start = (bf16[96,1536]{1,0:T(8,128)(2,1)}, bf16[96,1536]{1,0:T(8,128)(2,1)S(1)}, u32[]{:S(2)}) copy-start(bf16[96,1536]{1,0:T(8,128)(2,1)S(1)} %copy.31) | copy-start | bytes 884740
  115.9 18.9 %copy-start.3 = (f32[8]{0:T(128)S(1)}, f32[8]{0:T(128)}, u32[]{:S(2)}) copy-start(f32[8]{0:T(128)} %param.16) | copy-start | bytes 100
Sparse Core Ops, SparseCore 0:
  11.2 50.9 all-gather.3
  63.8 51.6 all-gather.5
  117.1 37.2 all-gather.7

commit v2 on v1

--- a/solution.py
+++ b/solution.py
@@ -1,22 +1,310 @@
 import jax
 import jax.numpy as jnp
 from jax import lax
+from jax.experimental import pallas as pl
+from jax.experimental.pallas import tpu as pltpu
 from jax.sharding import PartitionSpec as P
 
 HEAD_DIM = 128
-
-
-def with_halo(block, sides, width):
-    for axis, dim in sides:
-        count = lax.axis_size(axis)
-        forward = [(i, i + 1) for i in range(count - 1)]
-        backward = [(target, source) for source, target in forward]
-        low = lax.ppermute(
-            lax.slice_in_dim(block, block.shape[dim] - width, None, axis=dim), axis, forward
-        )
-        high = lax.ppermute(lax.slice_in_dim(block, 0, width, axis=dim), axis, backward)
-        block = jnp.concatenate([low, block, high], axis=dim)
-    return block
+MESH = pl.DeviceIdType.MESH
+MARGIN = 16
+EDGE = 8
+
+
+def flip(a, b):
+    low = lax.rem(lax.rem(a, 2) + lax.rem(b, 2), 2)
+    high = lax.rem(lax.div(a, 2) + lax.div(b, 2), 2)
+    return low + 2 * high
+
+
+def fused_kernel(
+    feat_ref, ngain_ref, cw_ref, bias_ref, again_ref, wq_ref, wkv_ref, scale_ref, wo_ref,
+    coarse_ref, attended_ref,
+    win, tmp0, tmp1, acc0, acc1, csend, cbuf, wqkv, wout, kvbuf,
+    act_send, act_recv, wa_send, wa_recv, wb_send, wb_recv, wc_send, wc_recv,
+    co_send, co_recv, kv_send, kv_recv,
+):
+    p = lax.axis_index("dp")
+    s = lax.axis_index("seq")
+    z, c = lax.div(s, 2), lax.rem(s, 2)
+    other = 1 - c
+    sibling = (p, 2 * z + other)
+    block = feat_ref.shape[0]
+    half = block // 2
+    heads = scale_ref.shape[0]
+    qcols = wq_ref.shape[1]
+    taps = cw_ref.shape[0]
+    width = cw_ref.shape[2]
+    depth = wq_ref.shape[0] // 4
+    odepth = wo_ref.shape[0] // 4
+
+    def remote(src, dst, send, recv, device):
+        return pltpu.make_async_remote_copy(
+            src_ref=src, dst_ref=dst, send_sem=send, recv_sem=recv,
+            device_id=device, device_id_type=MESH,
+        )
+
+    barrier = pltpu.get_barrier_semaphore()
+    for k in range(1, 8):
+        pl.semaphore_signal(
+            barrier, inc=1, device_id=(p, lax.rem(s + k, 8)), device_id_type=MESH
+        )
+    for k in range(1, 4):
+        pl.semaphore_signal(
+            barrier, inc=1, device_id=(lax.rem(p + k, 4), s), device_id_type=MESH
+        )
+    wqkv[c, z, :, :qcols] = wq_ref[...]
+    wqkv[c, z, :, qcols:] = wkv_ref[...]
+    wout[c, z] = wo_ref[...]
+    pl.semaphore_wait(barrier, 10)
+
+    started = []
+
+    def qkv_part(cc, zz, pp):
+        return wqkv.at[cc, zz, pl.ds(pl.multiple_of(pp * depth, 16), depth), :]
+
+    def out_part(cc, zz, pp):
+        return wout.at[cc, zz, pl.ds(pl.multiple_of(pp * odepth, 16), odepth), :]
+
+    for k in range(1, 4):
+        peer = (p, 2 * flip(z, k) + c)
+        for n, part in enumerate((qkv_part, out_part)):
+            copy = remote(
+                part(c, z, p), part(c, z, p), wa_send.at[n, k], wa_recv.at[n, z], peer
+            )
+            copy.start()
+            started.append(copy)
+
+    x = feat_ref[...].astype(jnp.float32)
+    meansq = jnp.mean(x * x, axis=-1, keepdims=True)
+    normed = x * lax.rsqrt(meansq + 1e-06) * ngain_ref[...]
+    win[s] = jax.nn.gelu(normed).astype(jnp.bfloat16)
+    for k in range(1, 4):
+        copy = remote(
+            win.at[s], win.at[s], act_send.at[k], act_recv.at[s], (p, 2 * flip(z, k) + c)
+        )
+        copy.start()
+        started.append(copy)
+    copy = remote(win.at[s], win.at[s], act_send.at[0], act_recv.at[s], sibling)
+    copy.start()
+    started.append(copy)
+
+    acc0[...] = jnp.zeros_like(acc0)
+    acc1[...] = jnp.zeros_like(acc1)
+    tmp0[...] = jnp.zeros_like(tmp0)
+    tmp1[...] = jnp.zeros_like(tmp1)
+
+    def convolve_block(b):
+        rows = win[b]
+        for t in range(taps):
+            y = jnp.dot(rows, cw_ref[t], preferred_element_type=jnp.float32)
+            tmp0[t, MARGIN : MARGIN + block, :] = y[:, :128]
+            tmp1[t, MARGIN : MARGIN + block, : width - 128] = y[:, 128:]
+        span = block + 2 * EDGE
+        first = MARGIN - EDGE - taps // 2
+        at = pl.ds(pl.multiple_of(b * block, 8), span)
+        for tmp, acc in ((tmp0, acc0), (tmp1, acc1)):
+            total = tmp[0, first : first + span, :]
+            for t in range(1, taps):
+                total = total + tmp[t, first + t : first + t + span, :]
+            acc[at, :] += total
+
+    def wait_block(b):
+        remote(win.at[b], win.at[b], act_send.at[0], act_recv.at[b], sibling).wait_recv()
+
+    convolve_block(s)
+    for k in range(1, 4):
+        zz = flip(z, k)
+        for n, part in enumerate((qkv_part, out_part)):
+            here = part(c, zz, p)
+            remote(here, here, wa_send.at[n, 0], wa_recv.at[n, zz], sibling).wait_recv()
+            for m in range(1, 4):
+                copy = remote(
+                    here, here, wb_send.at[n, k, m], wb_recv.at[n, zz, p],
+                    (lax.rem(p + m, 4), s),
+                )
+                copy.start()
+                started.append(copy)
+
+    def step(k, carry):
+        zz = flip(z, k)
+
+        @pl.when(k > 0)
+        def _():
+            b = 2 * zz + c
+            wait_block(b)
+            remote(
+                win.at[b], win.at[b], act_send.at[3 + k], act_recv.at[b], sibling
+            ).start()
+            convolve_block(b)
+
+        b = 2 * zz + other
+        wait_block(b)
+        convolve_block(b)
+        return carry
+
+    lax.fori_loop(0, 4, step, 0)
+
+    bias = bias_ref[s]
+
+    def pooled(r, out):
+        start = pl.multiple_of(r * block, 8) + EDGE
+        c0 = jnp.maximum(
+            acc0[pl.ds(start, half, stride=2), :], acc0[pl.ds(start + 1, half, stride=2), :]
+        )
+        c1 = jnp.maximum(
+            acc1[pl.ds(start, half, stride=2), :], acc1[pl.ds(start + 1, half, stride=2), :]
+        )
+        out[:, :128] = (c0 + bias[:, :128]).astype(jnp.bfloat16)
+        out[:, 128:] = (c1[:, : width - 128] + bias[:, 128:]).astype(jnp.bfloat16)
+
+    for k in range(1, 8):
+        r = lax.rem(s + k, 8)
+        pooled(r, csend.at[r])
+        copy = remote(csend.at[r], cbuf.at[s], co_send.at[k], co_recv.at[s], (p, r))
+        copy.start()
+        started.append(copy)
+    pooled(s, cbuf.at[s])
+
+    for k in range(1, 4):
+        zz = flip(z, k)
+        for n, part in enumerate((qkv_part, out_part)):
+            for m in range(1, 4):
+                pp = lax.rem(p + m, 4)
+                there = part(c, zz, pp)
+                remote(
+                    there, there, wa_send.at[n, 0], wb_recv.at[n, zz, pp], sibling
+                ).wait_recv()
+    for n, full in enumerate((wqkv, wout)):
+        copy = remote(full.at[c], full.at[c], wc_send.at[n], wc_recv.at[n], sibling)
+        copy.start()
+        started.append(copy)
+
+    for k in range(1, 8):
+        r = lax.rem(s + k, 8)
+        remote(csend.at[r], cbuf.at[r], co_send.at[0], co_recv.at[r], sibling).wait_recv()
+
+    squares = jnp.zeros((half, 1), jnp.float32)
+    for j in range(8):
+        piece = cbuf[j].astype(jnp.float32)
+        squares = squares + jnp.sum(piece * piece, axis=-1, keepdims=True)
+        coarse_ref[j] = cbuf[j]
+    inverse = lax.rsqrt(squares / (8 * width) + 1e-06)
+
+    remote(
+        wqkv.at[other], wqkv.at[other], wc_send.at[0], wc_recv.at[0], sibling
+    ).wait_recv()
+    attn = []
+    kv = jnp.zeros((half, wkv_ref.shape[1]), jnp.float32)
+    for j in range(8):
+        piece = (cbuf[j].astype(jnp.float32) * inverse * again_ref[j]).astype(jnp.bfloat16)
+        attn.append(piece)
+        kv = kv + jnp.dot(
+            piece, wqkv[j % 2, j // 2, :, qcols:], preferred_element_type=jnp.float32
+        )
+    kvbuf[s] = kv.astype(jnp.bfloat16)
+    for k in range(1, 8):
+        copy = remote(
+            kvbuf.at[s], kvbuf.at[s], kv_send.at[k], kv_recv.at[s], (p, lax.rem(s + k, 8))
+        )
+        copy.start()
+        started.append(copy)
+    query = jnp.zeros((half, qcols), jnp.float32)
+    for j in range(8):
+        query = query + jnp.dot(
+            attn[j], wqkv[j % 2, j // 2, :, :qcols], preferred_element_type=jnp.float32
+        )
+    query = query.astype(jnp.bfloat16)
+    remote(
+        wout.at[other], wout.at[other], wc_send.at[1], wc_recv.at[1], sibling
+    ).wait_recv()
+    for k in range(1, 8):
+        r = lax.rem(s + k, 8)
+        remote(kvbuf.at[r], kvbuf.at[r], kv_send.at[0], kv_recv.at[r], sibling).wait_recv()
+
+    keyvals = kvbuf[...].reshape(8 * half, kvbuf.shape[2])
+    keys, values = keyvals[:, :HEAD_DIM], keyvals[:, HEAD_DIM:]
+    result = jnp.zeros(attended_ref.shape, jnp.float32)
+    for h in range(heads):
+        scores = lax.dot_general(
+            query[:, h * HEAD_DIM : (h + 1) * HEAD_DIM], keys, (((1,), (1,)), ((), ())),
+            preferred_element_type=jnp.float32,
+        ) * (scale_ref[h] * HEAD_DIM ** (-0.5))
+        expon = jnp.exp(scores - jnp.max(scores, axis=1, keepdims=True))
+        denom = jnp.sum(expon, axis=1, keepdims=True)
+        context = jnp.dot(
+            expon.astype(jnp.bfloat16), values, preferred_element_type=jnp.float32
+        )
+        context = (context / denom).astype(jnp.bfloat16)
+        result = result + jnp.dot(
+            context, wout[h % 2, h // 2], preferred_element_type=jnp.float32
+        )
+    attended_ref[...] = result.astype(jnp.bfloat16)
+
+    for copy in started:
+        copy.wait_send()
+    for k in range(1, 4):
+        b = 2 * flip(z, k) + c
+        remote(
+            win.at[b], win.at[b], act_send.at[3 + k], act_recv.at[b], sibling
+        ).wait_send()
+
+
+def fused(
+    features, norm_gain, conv_weight, conv_bias, attn_gain,
+    query_weight, keyval_weight, head_scale, output_weight,
+):
+    block, channels = features.shape
+    half = block // 2
+    taps, _, width = conv_weight.shape
+    total = 8 * width
+    rows = 8 * block + 2 * EDGE
+    qkv_cols = query_weight.shape[1] + keyval_weight.shape[1]
+    f32, bf16 = jnp.float32, jnp.bfloat16
+    dma = pltpu.SemaphoreType.DMA
+    vmem = pl.BlockSpec(memory_space=pltpu.VMEM)
+    smem = pl.BlockSpec(memory_space=pltpu.SMEM)
+    coarse, attended = pl.pallas_call(
+        fused_kernel,
+        out_shape=(
+            jax.ShapeDtypeStruct((8, half, width), bf16),
+            jax.ShapeDtypeStruct((half, total), bf16),
+        ),
+        in_specs=[vmem] * 7 + [smem, vmem],
+        out_specs=(vmem, vmem),
+        scratch_shapes=[
+            pltpu.VMEM((8, block, channels), bf16),
+            pltpu.VMEM((taps, block + 2 * MARGIN, 128), f32),
+            pltpu.VMEM((taps, block + 2 * MARGIN, 128), f32),
+            pltpu.VMEM((rows, 128), f32),
+            pltpu.VMEM((rows, 128), f32),
+            pltpu.VMEM((8, half, width), bf16),
+            pltpu.VMEM((8, half, width), bf16),
+            pltpu.VMEM((2, 4, query_weight.shape[0], qkv_cols), bf16),
+            pltpu.VMEM((2, 4) + output_weight.shape, bf16),
+            pltpu.VMEM((8, half, keyval_weight.shape[1]), bf16),
+            dma((7,)), dma((8,)),
+            dma((2, 4)), dma((2, 4)),
+            dma((2, 4, 4)), dma((2, 4, 4)),
+            dma((2,)), dma((2,)),
+            dma((8,)), dma((8,)),
+            dma((8,)), dma((8,)),
+        ],
+        compiler_params=pltpu.CompilerParams(
+            collective_id=0, has_side_effects=True, vmem_limit_bytes=48 * 1024 * 1024
+        ),
+    )(
+        features,
+        norm_gain.reshape(1, channels),
+        conv_weight,
+        conv_bias.reshape(8, 1, width),
+        attn_gain.reshape(8, 1, width),
+        query_weight,
+        keyval_weight,
+        head_scale,
+        output_weight,
+    )
+    return coarse.transpose(1, 0, 2).reshape(half, total), attended
 
 
 def normalize(values_in, channel_gain):
@@ -108,8 +396,9 @@
 
 
 def solution(mesh):
+    fits = mesh.shape["dp"] == 4 and mesh.shape["seq"] == 8
     return jax.shard_map(
-        shards,
+        fused if fits else shards,
         mesh=mesh,
         in_specs=(
             P(("dp", "seq"), None),

time: 165 us -> 111 us (0.67)
  Pallas kernels: 0 us -> 96.8 us
  waiting for transfers between devices: 67.8 us -> 0 us
  blocking collectives: 50.8 us -> 0 us
  matrix products: 17.9 us -> 0 us
  between operations: 13.9 us -> 0.72 us
  local copies, waits for them, and re-layouts: 3.07 us -> 11.9 us
  other arithmetic: 7 us -> 0 us
  starting transfers between devices: 3.76 us -> 0 us
    pallas_call x0 -> x1, Pallas kernels: none -> 96.8 us  [fused(): pl.pallas_call(fused_kernel, out_shape=(jax.ShapeDtypeStruct((8, half, wi...]
    all_gather x3 -> x0, waiting for transfers between devices: 66.4 us -> none  [the longest x1 48.8 us: shards(): window = lax.all_gather(normed, 'seq', axis=0, tiled=True)]
    all_gather x2 -> x0, blocking collectives: 50.8 us -> none  [the longest x1 34.8 us: shards(): lax.all_gather(keyval_weight, 'seq', axis=0, tiled=True)]
    dot_general x10 -> x0, matrix products: 17.9 us -> none  [the longest x5 10.4 us: convolve(): jnp.dot(padded[kernel_tap:kernel_tap + row_count], kernel[kernel_tap], pr...]
    unnamed x12 -> x14, local copies, waits for them, and re-layouts: 0.03 us -> 8.26 us
    all_to_all x1 -> x0, starting transfers between devices: 3.64 us -> none  [shards(): lax.all_to_all(pooled, 'seq', split_axis=0, concat_axis=1, tiled=True)]
    reshape x1 -> x4, local copies, waits for them, and re-layouts: 0.39 us -> 3.4 us  [the longest x1 1.04 us: fused(): return (coarse.transpose(1, 0, 2).reshape(half, total), attended)]
    convert_element_type x1 -> x0, other arithmetic: 2.39 us -> none  [shards(): jax.nn.gelu(normalize(features.astype(jnp.float32), norm_gain))]
  transfers between devices with their start and end apart: 4 -> 0, of which waited for: 2 -> 0; matrix products, arithmetic and copies ran while one was open for 13% -> 0% of each run, Pallas kernels for 0% -> 0%
where the time goes in v2:
time: 111 us; the launch traced here: 109 us
  Pallas kernels  96.8 us (87%)
  local copies, waits for them, and re-layouts  11.9 us (11%)
    pallas_call x1, Pallas kernels, fused(): pl.pallas_call(fused_kernel, out_shape=(jax.ShapeDtypeStruct((8, half, wi...  96.8 us
    unnamed x14, local copies, waits for them, and re-layouts  8.26 us

profile of v2, /device:TPU:1, one launch (start us, length us, event | category | flops | bytes accessed | tf_op | source)
XLA Modules:
  0.0 109.4 jit_solution(4772540839207845030)
XLA Ops:
  0.6 0.0 copy-start.3
  0.6 0.0 copy-start.5
  0.7 0.0 copy-start.4
  0.7 0.0 copy-start.2
  0.7 0.0 copy-start.1
  0.7 0.8 reshape.16.ngain_ref
  1.5 0.8 reshape.17.bias_ref
  2.3 0.8 reshape.18.again_ref
  3.0 5.5 %copy.12.cw_ref = bf16[5,1408,192]{2,1,0:T(8,128)(2,1)} copy(bf16[5,1408,192]{1,2,0:T(8,128)(2,1)} %param.11) | data formatting | bytes 5406720 | tf_op args[2]
  8.6 0.0 copy-done.3
  8.6 0.0 copy-done.5
  8.6 0.0 copy-done.4
  8.6 0.0 copy-done.2
  8.6 0.0 copy-done.1
  8.6 0.0 copy-start
  8.6 2.0 %copy-done = bf16[5,1408,192]{2,1,0:T(8,128)(2,1)S(1)} copy-done((bf16[5,1408,192]{2,1,0:T(8,128)(2,1)S(1)}, bf16[5,1408,192]{2,1,0:T(8,128)(2,1)}, u32[]{:S(2)}) %copy-start) | copy-done | bytes 2703384
  10.6 96.8 %shard_map.104 = (bf16[8,96,192]{2,1,0:T(8,128)(2,1)S(1)}, bf16[96,1536]{1,0:T(8,128)(2,1)S(1)}) custom-call(bf16[192,1408]{1,0:T(8,128)(2,1)S(1)} %copy-done.1, f32[1,1408]{1,0:T(1,128)S(1)} %reshape.16.ngain_ref, bf16[5,1408,192]{2,1,0:T(8,128)(2,1)S(1)} %copy-done, f32[8,1,192]{2,1,0:T(1,128)S(1)} %reshape.17.bias_ref, ...), custom_call_target="tpu_custom_call" | custom-call | tf_op jit(solution)/shard_map/pallas_call | solution.py:267
  107.5 0.2 copy.13
  107.7 1.0 reshape.19
  108.7 0.7 copy.15
Async XLA Ops:
  0.6 7.9 %copy-start.3 = (bf16[128,1536]{1,0:T(8,128)(2,1)S(1)}, bf16[128,1536]{1,0:T(8,128)(2,1)}, u32[]{:S(2)}) copy-start(bf16[128,1536]{1,0:T(8,128)(2,1)} %wo_ref.1) | copy-start | bytes 1179652
  0.6 7.9 %copy-start.5 = (f32[8]{0:T(128)S(1)}, f32[8]{0:T(128)}, u32[]{:S(2)}) copy-start(f32[8]{0:T(128)} %scale_ref.1) | copy-start | bytes 100
  0.7 7.9 %copy-start.4 = (bf16[192,256]{1,0:T(8,128)(2,1)S(1)}, bf16[192,256]{1,0:T(8,128)(2,1)}, u32[]{:S(2)}) copy-start(bf16[192,256]{1,0:T(8,128)(2,1)} %wkv_ref.1) | copy-start | bytes 294916
  0.7 7.9 %copy-start.2 = (bf16[192,1024]{1,0:T(8,128)(2,1)S(1)}, bf16[192,1024]{1,0:T(8,128)(2,1)}, u32[]{:S(2)}) copy-start(bf16[192,1024]{1,0:T(8,128)(2,1)} %wq_ref.1) | copy-start | bytes 1179652
  0.7 7.9 %copy-start.1 = (bf16[192,1408]{1,0:T(8,128)(2,1)S(1)}, bf16[192,1408]{1,0:T(8,128)(2,1)}, u32[]{:S(2)}) copy-start(bf16[192,1408]{1,0:T(8,128)(2,1)} %feat_ref.1) | copy-start | bytes 1622020
  8.6 2.0 %copy-start = (bf16[5,1408,192]{2,1,0:T(8,128)(2,1)S(1)}, bf16[5,1408,192]{2,1,0:T(8,128)(2,1)}, u32[]{:S(2)}) copy-start(bf16[5,1408,192]{2,1,0:T(8,128)(2,1)} %copy.12.cw_ref) | copy-start | bytes 8110084

commit v3 on v2

--- a/solution.py
+++ b/solution.py
@@ -21,7 +21,7 @@
     feat_ref, ngain_ref, cw_ref, bias_ref, again_ref, wq_ref, wkv_ref, scale_ref, wo_ref,
     coarse_ref, attended_ref,
     win, tmp0, tmp1, acc0, acc1, csend, cbuf, wqkv, wout, kvbuf,
-    act_send, act_recv, wa_send, wa_recv, wb_send, wb_recv, wc_send, wc_recv,
+    bias8, again8, cw, scores_ref, prob_ref, cw_sem, act_send, act_recv, wa_send, wa_recv, wb_send, wb_recv, wc_send, wc_recv,
     co_send, co_recv, kv_send, kv_recv,
 ):
     p = lax.axis_index("dp")
@@ -34,7 +34,7 @@
     heads = scale_ref.shape[0]
     qcols = wq_ref.shape[1]
     taps = cw_ref.shape[0]
-    width = cw_ref.shape[2]
+    width = cw_ref.shape[1]
     depth = wq_ref.shape[0] // 4
     odepth = wo_ref.shape[0] // 4
 
@@ -44,6 +44,8 @@
             device_id=device, device_id_type=MESH,
         )
 
+    load = pltpu.make_async_copy(cw_ref, cw, cw_sem)
+    load.start()
     barrier = pltpu.get_barrier_semaphore()
     for k in range(1, 8):
         pl.semaphore_signal(
@@ -66,57 +68,21 @@
     def out_part(cc, zz, pp):
         return wout.at[cc, zz, pl.ds(pl.multiple_of(pp * odepth, 16), odepth), :]
 
-    for k in range(1, 4):
-        peer = (p, 2 * flip(z, k) + c)
-        for n, part in enumerate((qkv_part, out_part)):
+    parts = (qkv_part, out_part)
+
+    def along_z(n):
+        here = parts[n](c, z, p)
+        for k in range(1, 4):
             copy = remote(
-                part(c, z, p), part(c, z, p), wa_send.at[n, k], wa_recv.at[n, z], peer
+                here, here, wa_send.at[n, k], wa_recv.at[n, z], (p, 2 * flip(z, k) + c)
             )
             copy.start()
             started.append(copy)
 
-    x = feat_ref[...].astype(jnp.float32)
-    meansq = jnp.mean(x * x, axis=-1, keepdims=True)
-    normed = x * lax.rsqrt(meansq + 1e-06) * ngain_ref[...]
-    win[s] = jax.nn.gelu(normed).astype(jnp.bfloat16)
-    for k in range(1, 4):
-        copy = remote(
-            win.at[s], win.at[s], act_send.at[k], act_recv.at[s], (p, 2 * flip(z, k) + c)
-        )
-        copy.start()
-        started.append(copy)
-    copy = remote(win.at[s], win.at[s], act_send.at[0], act_recv.at[s], sibling)
-    copy.start()
-    started.append(copy)
-
-    acc0[...] = jnp.zeros_like(acc0)
-    acc1[...] = jnp.zeros_like(acc1)
-    tmp0[...] = jnp.zeros_like(tmp0)
-    tmp1[...] = jnp.zeros_like(tmp1)
-
-    def convolve_block(b):
-        rows = win[b]
-        for t in range(taps):
-            y = jnp.dot(rows, cw_ref[t], preferred_element_type=jnp.float32)
-            tmp0[t, MARGIN : MARGIN + block, :] = y[:, :128]
-            tmp1[t, MARGIN : MARGIN + block, : width - 128] = y[:, 128:]
-        span = block + 2 * EDGE
-        first = MARGIN - EDGE - taps // 2
-        at = pl.ds(pl.multiple_of(b * block, 8), span)
-        for tmp, acc in ((tmp0, acc0), (tmp1, acc1)):
-            total = tmp[0, first : first + span, :]
-            for t in range(1, taps):
-                total = total + tmp[t, first + t : first + t + span, :]
-            acc[at, :] += total
-
-    def wait_block(b):
-        remote(win.at[b], win.at[b], act_send.at[0], act_recv.at[b], sibling).wait_recv()
-
-    convolve_block(s)
-    for k in range(1, 4):
-        zz = flip(z, k)
-        for n, part in enumerate((qkv_part, out_part)):
-            here = part(c, zz, p)
+    def along_dp(n):
+        for k in range(1, 4):
+            zz = flip(z, k)
+            here = parts[n](c, zz, p)
             remote(here, here, wa_send.at[n, 0], wa_recv.at[n, zz], sibling).wait_recv()
             for m in range(1, 4):
                 copy = remote(
@@ -126,6 +92,67 @@
                 copy.start()
                 started.append(copy)
 
+    def along_core(n):
+        for k in range(1, 4):
+            zz = flip(z, k)
+            for m in range(1, 4):
+                pp = lax.rem(p + m, 4)
+                there = parts[n](c, zz, pp)
+                remote(
+                    there, there, wa_send.at[n, 0], wb_recv.at[n, zz, pp], sibling
+                ).wait_recv()
+        half_of = (wqkv, wout)[n].at[c]
+        copy = remote(half_of, half_of, wc_send.at[n], wc_recv.at[n], sibling)
+        copy.start()
+        started.append(copy)
+
+    along_z(0)
+
+    x = feat_ref[...].astype(jnp.float32)
+    meansq = jnp.mean(x * x, axis=-1, keepdims=True)
+    normed = x * lax.rsqrt(meansq + 1e-06) * ngain_ref[...][None, :]
+    win[s] = jax.nn.gelu(normed).astype(jnp.bfloat16)
+    for k in range(1, 4):
+        copy = remote(
+            win.at[s], win.at[s], act_send.at[k], act_recv.at[s], (p, 2 * flip(z, k) + c)
+        )
+        copy.start()
+        started.append(copy)
+    copy = remote(win.at[s], win.at[s], act_send.at[0], act_recv.at[s], sibling)
+    copy.start()
+    started.append(copy)
+
+    acc0[...] = jnp.zeros_like(acc0)
+    acc1[...] = jnp.zeros_like(acc1)
+    tmp0[...] = jnp.zeros_like(tmp0)
+    tmp1[...] = jnp.zeros_like(tmp1)
+
+    def convolve_pair(zz):
+        rows = win[pl.ds(2 * zz, 2)].reshape(2 * block, win.shape[2])
+        for t in range(taps):
+            y = lax.dot_general(
+                rows, cw[t], (((1,), (1,)), ((), ())), preferred_element_type=jnp.float32
+            )
+            tmp0[t, MARGIN : MARGIN + 2 * block, :] = y[:, :128]
+            tmp1[t, MARGIN : MARGIN + 2 * block, : width - 128] = y[:, 128:]
+        span = 2 * block + 2 * EDGE
+        first = MARGIN - EDGE - taps // 2
+        at = pl.ds(pl.multiple_of(zz * 2 * block, 8), span)
+        for tmp, acc in ((tmp0, acc0), (tmp1, acc1)):
+            total = tmp[0, first : first + span, :]
+            for t in range(1, taps):
+                total = total + tmp[t, first + t : first + t + span, :]
+            acc[at, :] += total
+
+    def wait_block(b):
+        remote(win.at[b], win.at[b], act_send.at[0], act_recv.at[b], sibling).wait_recv()
+
+    load.wait()
+    bias_row, again_row = bias_ref[...][None, :], again_ref[...][None, :]
+    for j in range(8):
+        bias8[j] = bias_row[:, j * width : (j + 1) * width]
+        again8[j] = again_row[:, j * width : (j + 1) * width]
+
     def step(k, carry):
         zz = flip(z, k)
 
@@ -136,16 +163,19 @@
             remote(
                 win.at[b], win.at[b], act_send.at[3 + k], act_recv.at[b], sibling
             ).start()
-            convolve_block(b)
-
-        b = 2 * zz + other
-        wait_block(b)
-        convolve_block(b)
+
+        wait_block(2 * zz + other)
+        convolve_pair(zz)
         return carry
 
-    lax.fori_loop(0, 4, step, 0)
-
-    bias = bias_ref[s]
+    lax.fori_loop(0, 1, step, 0)
+    along_dp(0)
+    lax.fori_loop(1, 3, step, 0)
+    along_z(1)
+    along_core(0)
+    lax.fori_loop(3, 4, step, 0)
+
+    bias = bias8[s]
 
     def pooled(r, out):
         start = pl.multiple_of(r * block, 8) + EDGE
@@ -166,20 +196,7 @@
         started.append(copy)
     pooled(s, cbuf.at[s])
 
-    for k in range(1, 4):
-        zz = flip(z, k)
-        for n, part in enumerate((qkv_part, out_part)):
-            for m in range(1, 4):
-                pp = lax.rem(p + m, 4)
-                there = part(c, zz, pp)
-                remote(
-                    there, there, wa_send.at[n, 0], wb_recv.at[n, zz, pp], sibling
-                ).wait_recv()
-    for n, full in enumerate((wqkv, wout)):
-        copy = remote(full.at[c], full.at[c], wc_send.at[n], wc_recv.at[n], sibling)
-        copy.start()
-        started.append(copy)
-
+    along_dp(1)
     for k in range(1, 8):
         r = lax.rem(s + k, 8)
         remote(csend.at[r], cbuf.at[r], co_send.at[0], co_recv.at[r], sibling).wait_recv()
@@ -197,49 +214,69 @@
     attn = []
     kv = jnp.zeros((half, wkv_ref.shape[1]), jnp.float32)
     for j in range(8):
-        piece = (cbuf[j].astype(jnp.float32) * inverse * again_ref[j]).astype(jnp.bfloat16)
+        piece = (cbuf[j].astype(jnp.float32) * inverse * again8[j]).astype(jnp.bfloat16)
         attn.append(piece)
         kv = kv + jnp.dot(
             piece, wqkv[j % 2, j // 2, :, qcols:], preferred_element_type=jnp.float32
         )
     kvbuf[s] = kv.astype(jnp.bfloat16)
-    for k in range(1, 8):
+    for k in range(1, 4):
         copy = remote(
-            kvbuf.at[s], kvbuf.at[s], kv_send.at[k], kv_recv.at[s], (p, lax.rem(s + k, 8))
+            kvbuf.at[s], kvbuf.at[s], kv_send.at[k], kv_recv.at[s], (p, 2 * flip(z, k) + c)
         )
         copy.start()
         started.append(copy)
+    copy = remote(kvbuf.at[s], kvbuf.at[s], kv_send.at[0], kv_recv.at[s], sibling)
+    copy.start()
+    started.append(copy)
     query = jnp.zeros((half, qcols), jnp.float32)
     for j in range(8):
         query = query + jnp.dot(
             attn[j], wqkv[j % 2, j // 2, :, :qcols], preferred_element_type=jnp.float32
         )
     query = query.astype(jnp.bfloat16)
+    stacked = jnp.concatenate(
+        [query[:, h * HEAD_DIM : (h + 1) * HEAD_DIM] for h in range(heads)], axis=0
+    )
+    for k in range(1, 4):
+        b = 2 * flip(z, k) + c
+        remote(kvbuf.at[b], kvbuf.at[b], kv_send.at[0], kv_recv.at[b], sibling).wait_recv()
+        copy = remote(kvbuf.at[b], kvbuf.at[b], kv_send.at[3 + k], kv_recv.at[b], sibling)
+        copy.start()
+        started.append(copy)
+    along_core(1)
+    for k in range(4):
+        b = 2 * flip(z, k) + other
+        remote(kvbuf.at[b], kvbuf.at[b], kv_send.at[0], kv_recv.at[b], sibling).wait_recv()
+
+    keyvals = kvbuf[...].reshape(8 * half, kvbuf.shape[2])
+    keys, values = keyvals[:, :HEAD_DIM], keyvals[:, HEAD_DIM:]
+    scores_ref[...] = lax.dot_general(
+        stacked, keys, (((1,), (1,)), ((), ())), preferred_element_type=jnp.float32
+    )
+    denoms = []
+    for h in range(heads):
+        at = slice(h * half, (h + 1) * half)
+        scores = scores_ref[at, :] * (scale_ref[h] * HEAD_DIM ** (-0.5))
+        expon = jnp.exp(scores - jnp.max(scores, axis=1, keepdims=True))
+        denoms.append(jnp.sum(expon, axis=1, keepdims=True))
+        prob_ref[at, :] = expon.astype(jnp.bfloat16)
+    context = jnp.dot(prob_ref[...], values, preferred_element_type=jnp.float32)
+    context = jnp.concatenate(
+        [
+            (context[h * half : (h + 1) * half] / denoms[h]).astype(jnp.bfloat16)
+            for h in [2 * zz + cc for cc in range(2) for zz in range(heads // 2)]
+        ],
+        axis=1,
+    )
     remote(
         wout.at[other], wout.at[other], wc_send.at[1], wc_recv.at[1], sibling
     ).wait_recv()
-    for k in range(1, 8):
-        r = lax.rem(s + k, 8)
-        remote(kvbuf.at[r], kvbuf.at[r], kv_send.at[0], kv_recv.at[r], sibling).wait_recv()
-
-    keyvals = kvbuf[...].reshape(8 * half, kvbuf.shape[2])
-    keys, values = keyvals[:, :HEAD_DIM], keyvals[:, HEAD_DIM:]
-    result = jnp.zeros(attended_ref.shape, jnp.float32)
-    for h in range(heads):
-        scores = lax.dot_general(
-            query[:, h * HEAD_DIM : (h + 1) * HEAD_DIM], keys, (((1,), (1,)), ((), ())),
-            preferred_element_type=jnp.float32,
-        ) * (scale_ref[h] * HEAD_DIM ** (-0.5))
-        expon = jnp.exp(scores - jnp.max(scores, axis=1, keepdims=True))
-        denom = jnp.sum(expon, axis=1, keepdims=True)
-        context = jnp.dot(
-            expon.astype(jnp.bfloat16), values, preferred_element_type=jnp.float32
-        )
-        context = (context / denom).astype(jnp.bfloat16)
-        result = result + jnp.dot(
-            context, wout[h % 2, h // 2], preferred_element_type=jnp.float32
-        )
-    attended_ref[...] = result.astype(jnp.bfloat16)
+    attended_ref[...] = jnp.dot(
+        context,
+        wout[...].reshape(heads * HEAD_DIM, attended_ref.shape[1]),
+        preferred_element_type=jnp.float32,
+    ).astype(jnp.bfloat16)
 
     for copy in started:
         copy.wait_send()
@@ -257,6 +294,7 @@
     block, channels = features.shape
     half = block // 2
     taps, _, width = conv_weight.shape
+    heads = head_scale.shape[0]
     total = 8 * width
     rows = 8 * block + 2 * EDGE
     qkv_cols = query_weight.shape[1] + keyval_weight.shape[1]
@@ -270,12 +308,12 @@
             jax.ShapeDtypeStruct((8, half, width), bf16),
             jax.ShapeDtypeStruct((half, total), bf16),
         ),
-        in_specs=[vmem] * 7 + [smem, vmem],
+        in_specs=[vmem, vmem, pl.BlockSpec(memory_space=pl.ANY)] + [vmem] * 4 + [smem, vmem],
         out_specs=(vmem, vmem),
         scratch_shapes=[
             pltpu.VMEM((8, block, channels), bf16),
-            pltpu.VMEM((taps, block + 2 * MARGIN, 128), f32),
-            pltpu.VMEM((taps, block + 2 * MARGIN, 128), f32),
+            pltpu.VMEM((taps, 2 * block + 2 * MARGIN, 128), f32),
+            pltpu.VMEM((taps, 2 * block + 2 * MARGIN, 128), f32),
             pltpu.VMEM((rows, 128), f32),
             pltpu.VMEM((rows, 128), f32),
             pltpu.VMEM((8, half, width), bf16),
@@ -283,6 +321,12 @@
             pltpu.VMEM((2, 4, query_weight.shape[0], qkv_cols), bf16),
             pltpu.VMEM((2, 4) + output_weight.shape, bf16),
             pltpu.VMEM((8, half, keyval_weight.shape[1]), bf16),
+            pltpu.VMEM((8, 1, width), f32),
+            pltpu.VMEM((8, 1, width), f32),
+            pltpu.VMEM((taps, width, channels), bf16),
+            pltpu.VMEM((heads * half, 8 * half), f32),
+            pltpu.VMEM((heads * half, 8 * half), bf16),
+            dma(()),
             dma((7,)), dma((8,)),
             dma((2, 4)), dma((2, 4)),
             dma((2, 4, 4)), dma((2, 4, 4)),
@@ -291,14 +335,14 @@
             dma((8,)), dma((8,)),
         ],
         compiler_params=pltpu.CompilerParams(
-            collective_id=0, has_side_effects=True, vmem_limit_bytes=48 * 1024 * 1024
+            collective_id=0, has_side_effects=True, vmem_limit_bytes=60 * 1024 * 1024
         ),
     )(
         features,
-        norm_gain.reshape(1, channels),
-        conv_weight,
-        conv_bias.reshape(8, 1, width),
-        attn_gain.reshape(8, 1, width),
+        norm_gain,
+        conv_weight.transpose(0, 2, 1),
+        conv_bias,
+        attn_gain,
         query_weight,
         keyval_weight,
         head_scale,

time: 111 us -> 101 us (0.910)
  local copies, waits for them, and re-layouts: 11.9 us -> 3.94 us
    unnamed x14 -> x1, local copies, waits for them, and re-layouts: 8.26 us -> 1.69 us
    reshape x3 -> x0, local copies, waits for them, and re-layouts: 2.36 us -> none  [the longest x1 0.8 us: fused(): norm_gain.reshape(1, channels)]
where the time goes in v3:
time: 101 us
  Pallas kernels  95.9 us (95%)
  local copies, waits for them, and re-layouts  3.94 us (4%)
    pallas_call x1, Pallas kernels, fused(): pl.pallas_call(fused_kernel, out_shape=(jax.ShapeDtypeStruct((8, half, wi...  95.9 us

profile of v3, /device:TPU:1, one launch (start us, length us, event | category | flops | bytes accessed | tf_op | source)
XLA Modules:
  0.0 100.5 jit_solution(16760831159462821521)
XLA Ops:
  0.6 95.9 %shard_map.104 = (bf16[8,96,192]{2,1,0:T(8,128)(2,1)}, bf16[96,1536]{1,0:T(8,128)(2,1)}) custom-call(bf16[192,1408]{1,0:T(8,128)(2,1)} %feat_ref.1, f32[1408]{0:T(1024)} %ngain_ref.1, bf16[5,192,1408]{2,1,0:T(8,128)(2,1)} %bitcast.2, f32[1536]{0:T(1024)} %bias_ref.1, f32[1536]{0:T(1024)} %again_ref.1, bf16[192,1024]{1,0:T(8,128)(2,1)} %wq_ref.1, ...), custom_call_target="tpu_custom_call" | custom-call | tf_op jit(solution)/shard_map/pallas_call | solution.py:305
  96.6 1.2 %copy.11 = bf16[96,8,192]{2,1,0:T(8,128)(2,1)S(1)} copy(bf16[96,8,192]{2,0,1:T(8,128)(2,1)} %bitcast.3) | data formatting | bytes 589824 | tf_op jit(solution)/shard_map/transpose | solution.py:351
  97.8 1.0 %reshape.7 = bf16[96,1536]{1,0:T(8,128)(2,1)} reshape(bf16[96,8,192]{2,1,0:T(8,128)(2,1)S(1)} %copy.11) | data formatting | bytes 589824 | tf_op jit(solution)/shard_map/reshape | solution.py:351
  98.8 1.7 %copy.13 = bf16[96,1536]{1,0:T(8,128)(2,1)} copy(bf16[96,1536]{1,0:T(8,128)(2,1)} %get-tuple-element.9) | data formatting | bytes 589824

commit v4 on v3

--- a/solution.py
+++ b/solution.py
@@ -11,17 +11,20 @@
 EDGE = 8
 
 
-def flip(a, b):
-    low = lax.rem(lax.rem(a, 2) + lax.rem(b, 2), 2)
-    high = lax.rem(lax.div(a, 2) + lax.div(b, 2), 2)
-    return low + 2 * high
+def nearest(z, k):
+    upper = lax.div(z, 2)
+    if k == 0:
+        return z
+    if k == 1:
+        return z + 1 - 2 * lax.rem(z, 2)
+    return k - upper * (2 * k - 3)
 
 
 def fused_kernel(
     feat_ref, ngain_ref, cw_ref, bias_ref, again_ref, wq_ref, wkv_ref, scale_ref, wo_ref,
     coarse_ref, attended_ref,
     win, tmp0, tmp1, acc0, acc1, csend, cbuf, wqkv, wout, kvbuf,
-    bias8, again8, cw, scores_ref, prob_ref, cw_sem, act_send, act_recv, wa_send, wa_recv, wb_send, wb_recv, wc_send, wc_recv,
+    bias8, again8, cw, cwt, scores_ref, prob_ref, cw_sem, act_send, act_recv, wa_send, wa_recv, wb_send, wb_recv, wc_send, wc_recv,
     co_send, co_recv, kv_send, kv_recv,
 ):
     p = lax.axis_index("dp")
@@ -74,14 +77,14 @@
         here = parts[n](c, z, p)
         for k in range(1, 4):
             copy = remote(
-                here, here, wa_send.at[n, k], wa_recv.at[n, z], (p, 2 * flip(z, k) + c)
+                here, here, wa_send.at[n, k], wa_recv.at[n, z], (p, 2 * nearest(z, k) + c)
             )
             copy.start()
             started.append(copy)
 
     def along_dp(n):
         for k in range(1, 4):
-            zz = flip(z, k)
+            zz = nearest(z, k)
             here = parts[n](c, zz, p)
             remote(here, here, wa_send.at[n, 0], wa_recv.at[n, zz], sibling).wait_recv()
             for m in range(1, 4):
@@ -94,7 +97,7 @@
 
     def along_core(n):
         for k in range(1, 4):
-            zz = flip(z, k)
+            zz = nearest(z, k)
             for m in range(1, 4):
                 pp = lax.rem(p + m, 4)
                 there = parts[n](c, zz, pp)
@@ -114,7 +117,7 @@
     win[s] = jax.nn.gelu(normed).astype(jnp.bfloat16)
     for k in range(1, 4):
         copy = remote(
-            win.at[s], win.at[s], act_send.at[k], act_recv.at[s], (p, 2 * flip(z, k) + c)
+            win.at[s], win.at[s], act_send.at[k], act_recv.at[s], (p, 2 * nearest(z, k) + c)
         )
         copy.start()
         started.append(copy)
@@ -130,9 +133,7 @@
     def convolve_pair(zz):
         rows = win[pl.ds(2 * zz, 2)].reshape(2 * block, win.shape[2])
         for t in range(taps):
-            y = lax.dot_general(
-                rows, cw[t], (((1,), (1,)), ((), ())), preferred_element_type=jnp.float32
-            )
+            y = jnp.dot(rows, cwt[t], preferred_element_type=jnp.float32)
             tmp0[t, MARGIN : MARGIN + 2 * block, :] = y[:, :128]
             tmp1[t, MARGIN : MARGIN + 2 * block, : width - 128] = y[:, 128:]
         span = 2 * block + 2 * EDGE
@@ -148,64 +149,73 @@
         remote(win.at[b], win.at[b], act_send.at[0], act_recv.at[b], sibling).wait_recv()
 
     load.wait()
+    for t in range(taps):
+        cwt[t] = cw[t].T
     bias_row, again_row = bias_ref[...][None, :], again_ref[...][None, :]
     for j in range(8):
         bias8[j] = bias_row[:, j * width : (j + 1) * width]
         again8[j] = again_row[:, j * width : (j + 1) * width]
 
-    def step(k, carry):
-        zz = flip(z, k)
-
-        @pl.when(k > 0)
-        def _():
+    def step(k):
+        zz = nearest(z, k)
+        if k > 0:
             b = 2 * zz + c
             wait_block(b)
-            remote(
+            copy = remote(
                 win.at[b], win.at[b], act_send.at[3 + k], act_recv.at[b], sibling
-            ).start()
-
+            )
+            copy.start()
+            started.append(copy)
         wait_block(2 * zz + other)
         convolve_pair(zz)
-        return carry
-
-    lax.fori_loop(0, 1, step, 0)
-    along_dp(0)
-    lax.fori_loop(1, 3, step, 0)
-    along_z(1)
-    along_core(0)
-    lax.fori_loop(3, 4, step, 0)
-
-    bias = bias8[s]
 
     def pooled(r, out):
         start = pl.multiple_of(r * block, 8) + EDGE
+        bias = bias8[s]
         c0 = jnp.maximum(
             acc0[pl.ds(start, half, stride=2), :], acc0[pl.ds(start + 1, half, stride=2), :]
         )
         c1 = jnp.maximum(
             acc1[pl.ds(start, half, stride=2), :], acc1[pl.ds(start + 1, half, stride=2), :]
         )
-        out[:, :128] = (c0 + bias[:, :128]).astype(jnp.bfloat16)
-        out[:, 128:] = (c1[:, : width - 128] + bias[:, 128:]).astype(jnp.bfloat16)
-
-    for k in range(1, 8):
-        r = lax.rem(s + k, 8)
+        c1 = (c1[:, : width - 128] + bias[:, 128:]).astype(jnp.bfloat16)
+        out[:half, :] = (c0 + bias[:, :128]).astype(jnp.bfloat16)
+        out[half:, :64] = c1[: half // 2]
+        out[half:, 64:] = c1[half // 2 :]
+
+    def send_rows(k, r):
         pooled(r, csend.at[r])
         copy = remote(csend.at[r], cbuf.at[s], co_send.at[k], co_recv.at[s], (p, r))
         copy.start()
         started.append(copy)
+
+    step(0)
+    along_dp(0)
+    step(1)
+    along_z(1)
+    step(2)
+    upper = lax.div(z, 2)
+    send_rows(4, 4 - upper)
+    for k in range(1, 4):
+        send_rows(k, 4 * upper + lax.rem(s + k, 4))
     pooled(s, cbuf.at[s])
-
+    along_core(0)
+    step(3)
+    for k in range(5, 8):
+        send_rows(k, k + upper * (7 - 2 * k))
     along_dp(1)
     for k in range(1, 8):
         r = lax.rem(s + k, 8)
         remote(csend.at[r], cbuf.at[r], co_send.at[0], co_recv.at[r], sibling).wait_recv()
 
     squares = jnp.zeros((half, 1), jnp.float32)
+    pieces = []
     for j in range(8):
-        piece = cbuf[j].astype(jnp.float32)
+        narrow = jnp.concatenate([cbuf[j, half:, :64], cbuf[j, half:, 64:]], axis=0)
+        piece = jnp.concatenate([cbuf[j, :half, :], narrow], axis=1)
+        pieces.append(piece)
+        piece = piece.astype(jnp.float32)
         squares = squares + jnp.sum(piece * piece, axis=-1, keepdims=True)
-        coarse_ref[j] = cbuf[j]
     inverse = lax.rsqrt(squares / (8 * width) + 1e-06)
 
     remote(
@@ -214,7 +224,7 @@
     attn = []
     kv = jnp.zeros((half, wkv_ref.shape[1]), jnp.float32)
     for j in range(8):
-        piece = (cbuf[j].astype(jnp.float32) * inverse * again8[j]).astype(jnp.bfloat16)
+        piece = (pieces[j].astype(jnp.float32) * inverse * again8[j]).astype(jnp.bfloat16)
         attn.append(piece)
         kv = kv + jnp.dot(
             piece, wqkv[j % 2, j // 2, :, qcols:], preferred_element_type=jnp.float32
@@ -222,13 +232,15 @@
     kvbuf[s] = kv.astype(jnp.bfloat16)
     for k in range(1, 4):
         copy = remote(
-            kvbuf.at[s], kvbuf.at[s], kv_send.at[k], kv_recv.at[s], (p, 2 * flip(z, k) + c)
+            kvbuf.at[s], kvbuf.at[s], kv_send.at[k], kv_recv.at[s], (p, 2 * nearest(z, k) + c)
         )
         copy.start()
         started.append(copy)
     copy = remote(kvbuf.at[s], kvbuf.at[s], kv_send.at[0], kv_recv.at[s], sibling)
     copy.start()
     started.append(copy)
+    for j in range(8):
+        coarse_ref[:, j * width : (j + 1) * width] = pieces[j]
     query = jnp.zeros((half, qcols), jnp.float32)
     for j in range(8):
         query = query + jnp.dot(
@@ -239,14 +251,14 @@
         [query[:, h * HEAD_DIM : (h + 1) * HEAD_DIM] for h in range(heads)], axis=0
     )
     for k in range(1, 4):
-        b = 2 * flip(z, k) + c
+        b = 2 * nearest(z, k) + c
         remote(kvbuf.at[b], kvbuf.at[b], kv_send.at[0], kv_recv.at[b], sibling).wait_recv()
         copy = remote(kvbuf.at[b], kvbuf.at[b], kv_send.at[3 + k], kv_recv.at[b], sibling)
         copy.start()
         started.append(copy)
     along_core(1)
     for k in range(4):
-        b = 2 * flip(z, k) + other
+        b = 2 * nearest(z, k) + other
         remote(kvbuf.at[b], kvbuf.at[b], kv_send.at[0], kv_recv.at[b], sibling).wait_recv()
 
     keyvals = kvbuf[...].reshape(8 * half, kvbuf.shape[2])
@@ -280,11 +292,6 @@
 
     for copy in started:
         copy.wait_send()
-    for k in range(1, 4):
-        b = 2 * flip(z, k) + c
-        remote(
-            win.at[b], win.at[b], act_send.at[3 + k], act_recv.at[b], sibling
-        ).wait_send()
 
 
 def fused(
@@ -305,7 +312,7 @@
     coarse, attended = pl.pallas_call(
         fused_kernel,
         out_shape=(
-            jax.ShapeDtypeStruct((8, half, width), bf16),
+            jax.ShapeDtypeStruct((half, total), bf16),
             jax.ShapeDtypeStruct((half, total), bf16),
         ),
         in_specs=[vmem, vmem, pl.BlockSpec(memory_space=pl.ANY)] + [vmem] * 4 + [smem, vmem],
@@ -316,14 +323,15 @@
             pltpu.VMEM((taps, 2 * block + 2 * MARGIN, 128), f32),
             pltpu.VMEM((rows, 128), f32),
             pltpu.VMEM((rows, 128), f32),
-            pltpu.VMEM((8, half, width), bf16),
-            pltpu.VMEM((8, half, width), bf16),
+            pltpu.VMEM((8, half + half // 2, 128), bf16),
+            pltpu.VMEM((8, half + half // 2, 128), bf16),
             pltpu.VMEM((2, 4, query_weight.shape[0], qkv_cols), bf16),
             pltpu.VMEM((2, 4) + output_weight.shape, bf16),
             pltpu.VMEM((8, half, keyval_weight.shape[1]), bf16),
             pltpu.VMEM((8, 1, width), f32),
             pltpu.VMEM((8, 1, width), f32),
             pltpu.VMEM((taps, width, channels), bf16),
+            pltpu.VMEM((taps, channels, width), bf16),
             pltpu.VMEM((heads * half, 8 * half), f32),
             pltpu.VMEM((heads * half, 8 * half), bf16),
             dma(()),
@@ -348,7 +356,7 @@
         head_scale,
         output_weight,
     )
-    return coarse.transpose(1, 0, 2).reshape(half, total), attended
+    return coarse, attended
 
 
 def normalize(values_in, channel_gain):

time: 101 us -> 105 us (1.040)
  Pallas kernels: 95.9 us -> 101 us
    pallas_call x1, Pallas kernels: 95.9 us -> 101 us  [fused(): pl.pallas_call(fused_kernel, out_shape=(jax.ShapeDtypeStruct((half, total...]
    unnamed x1 -> x2, local copies, waits for them, and re-layouts: 1.69 us -> 3.39 us
    transpose x1 -> x0, local copies, waits for them, and re-layouts: 1.22 us -> none  [fused(): return (coarse.transpose(1, 0, 2).reshape(half, total), attended)]
where the time goes in v4:
time: 105 us
  Pallas kernels  101 us (96%)
  local copies, waits for them, and re-layouts  3.39 us (3%)
    pallas_call x1, Pallas kernels, fused(): pl.pallas_call(fused_kernel, out_shape=(jax.ShapeDtypeStruct((half, total...  101 us
    unnamed x2, local copies, waits for them, and re-layouts  3.39 us

profile of v4, /device:TPU:1, one launch (start us, length us, event | category | flops | bytes accessed | tf_op | source)
XLA Modules:
  0.0 104.8 jit_solution(7176800143894441016)
XLA Ops:
  0.6 100.7 %shard_map.104 = (bf16[96,1536]{1,0:T(8,128)(2,1)}, bf16[96,1536]{1,0:T(8,128)(2,1)}) custom-call(bf16[192,1408]{1,0:T(8,128)(2,1)} %feat_ref.1, f32[1408]{0:T(1024)} %ngain_ref.1, bf16[5,192,1408]{2,1,0:T(8,128)(2,1)} %bitcast.1, f32[1536]{0:T(1024)} %bias_ref.1, f32[1536]{0:T(1024)} %again_ref.1, bf16[192,1024]{1,0:T(8,128)(2,1)} %wq_ref.1, ...), custom_call_target="tpu_custom_call" | custom-call | tf_op jit(solution)/shard_map/pallas_call | solution.py:312
  101.4 1.7 %copy.13 = bf16[96,1536]{1,0:T(8,128)(2,1)} copy(bf16[96,1536]{1,0:T(8,128)(2,1)} %get-tuple-element.4) | data formatting | bytes 589824
  103.1 1.7 %copy.14 = bf16[96,1536]{1,0:T(8,128)(2,1)} copy(bf16[96,1536]{1,0:T(8,128)(2,1)} %get-tuple-element.5) | data formatting | bytes 589824

commit v5 on v4

--- a/solution.py
+++ b/solution.py
@@ -72,10 +72,21 @@
         return wout.at[cc, zz, pl.ds(pl.multiple_of(pp * odepth, 16), odepth), :]
 
     parts = (qkv_part, out_part)
+    middle = lax.rem(lax.div(z + 1, 2), 2) == 1
+    end = (p, 2 * nearest(z, 1) + c)
+    relays = []
+
+    def relay(ref, send, recv):
+        copy = remote(ref, ref, send, recv, end)
+        relays.append(copy)
+
+        @pl.when(middle)
+        def _():
+            copy.start()
 
     def along_z(n):
         here = parts[n](c, z, p)
-        for k in range(1, 4):
+        for k in range(1, 3):
             copy = remote(
                 here, here, wa_send.at[n, k], wa_recv.at[n, z], (p, 2 * nearest(z, k) + c)
             )
@@ -87,6 +98,8 @@
             zz = nearest(z, k)
             here = parts[n](c, zz, p)
             remote(here, here, wa_send.at[n, 0], wa_recv.at[n, zz], sibling).wait_recv()
+            if k > 1:
+                relay(here, wa_send.at[n, 1 + k], wa_recv.at[n, zz])
             for m in range(1, 4):
                 copy = remote(
                     here, here, wb_send.at[n, k, m], wb_recv.at[n, zz, p],
@@ -115,7 +128,7 @@
     meansq = jnp.mean(x * x, axis=-1, keepdims=True)
     normed = x * lax.rsqrt(meansq + 1e-06) * ngain_ref[...][None, :]
     win[s] = jax.nn.gelu(normed).astype(jnp.bfloat16)
-    for k in range(1, 4):
+    for k in range(1, 3):
         copy = remote(
             win.at[s], win.at[s], act_send.at[k], act_recv.at[s], (p, 2 * nearest(z, k) + c)
         )
@@ -164,8 +177,12 @@
             copy = remote(
                 win.at[b], win.at[b], act_send.at[3 + k], act_recv.at[b], sibling
             )
+            if k > 1:
+                relay(win.at[b], act_send.at[5 + k], act_recv.at[b])
             copy.start()
             started.append(copy)
+        if k == 3:
+            along_dp(1)
         wait_block(2 * zz + other)
         convolve_pair(zz)
 
@@ -203,7 +220,6 @@
     step(3)
     for k in range(5, 8):
         send_rows(k, k + upper * (7 - 2 * k))
-    along_dp(1)
     for k in range(1, 8):
         r = lax.rem(s + k, 8)
         remote(csend.at[r], cbuf.at[r], co_send.at[0], co_recv.at[r], sibling).wait_recv()
@@ -292,6 +308,11 @@
 
     for copy in started:
         copy.wait_send()
+
+    @pl.when(middle)
+    def _():
+        for copy in relays:
+            copy.wait_send()
 
 
 def fused(
@@ -335,8 +356,8 @@
             pltpu.VMEM((heads * half, 8 * half), f32),
             pltpu.VMEM((heads * half, 8 * half), bf16),
             dma(()),
-            dma((7,)), dma((8,)),
-            dma((2, 4)), dma((2, 4)),
+            dma((9,)), dma((8,)),
+            dma((2, 5)), dma((2, 4)),
             dma((2, 4, 4)), dma((2, 4, 4)),
             dma((2,)), dma((2,)),
             dma((8,)), dma((8,)),

time: 105 us -> 88.4 us (0.84)
  Pallas kernels: 101 us -> 84.2 us
    pallas_call x1, Pallas kernels: 101 us -> 84.2 us  [fused(): pl.pallas_call(fused_kernel, out_shape=(jax.ShapeDtypeStruct((half, total...]
where the time goes in v5:
time: 88.4 us; the launch traced here: 88.2 us
  Pallas kernels  84.2 us (95%)
  local copies, waits for them, and re-layouts  3.39 us (4%)
    pallas_call x1, Pallas kernels, fused(): pl.pallas_call(fused_kernel, out_shape=(jax.ShapeDtypeStruct((half, total...  84.2 us
    unnamed x2, local copies, waits for them, and re-layouts  3.39 us

profile of v5, /device:TPU:1, one launch (start us, length us, event | category | flops | bytes accessed | tf_op | source)
XLA Modules:
  0.0 88.2 jit_solution(14300212452800034510)
XLA Ops:
  0.6 84.2 %shard_map.104 = (bf16[96,1536]{1,0:T(8,128)(2,1)}, bf16[96,1536]{1,0:T(8,128)(2,1)}) custom-call(bf16[192,1408]{1,0:T(8,128)(2,1)} %feat_ref.1, f32[1408]{0:T(1024)} %ngain_ref.1, bf16[5,192,1408]{2,1,0:T(8,128)(2,1)} %bitcast.1, f32[1536]{0:T(1024)} %bias_ref.1, f32[1536]{0:T(1024)} %again_ref.1, bf16[192,1024]{1,0:T(8,128)(2,1)} %wq_ref.1, ...), custom_call_target="tpu_custom_call" | custom-call | tf_op jit(solution)/shard_map/pallas_call | solution.py:333
  84.8 1.7 %copy.13 = bf16[96,1536]{1,0:T(8,128)(2,1)} copy(bf16[96,1536]{1,0:T(8,128)(2,1)} %get-tuple-element.4) | data formatting | bytes 589824
  86.5 1.7 %copy.14 = bf16[96,1536]{1,0:T(8,128)(2,1)} copy(bf16[96,1536]{1,0:T(8,128)(2,1)} %get-tuple-element.5) | data formatting | bytes 589824

commit v6 on v5

--- a/solution.py
+++ b/solution.py
@@ -11,13 +11,18 @@
 EDGE = 8
 
 
-def nearest(z, k):
-    upper = lax.div(z, 2)
+def beside(z):
+    return z + 1 - 2 * lax.rem(z, 2)
+
+
+def visit(z, k):
     if k == 0:
         return z
     if k == 1:
-        return z + 1 - 2 * lax.rem(z, 2)
-    return k - upper * (2 * k - 3)
+        return 1 + lax.rem(z, 2)
+    if k == 2:
+        return lax.rem(2 + 3 * z, 5)
+    return 3 * (1 - lax.div(z, 2))
 
 
 def fused_kernel(
@@ -73,33 +78,30 @@
 
     parts = (qkv_part, out_part)
     middle = lax.rem(lax.div(z + 1, 2), 2) == 1
-    end = (p, 2 * nearest(z, 1) + c)
-    relays = []
+    end = (p, 2 * beside(z) + c)
+    targets = (2 - lax.div(z, 2), beside(z))
 
     def relay(ref, send, recv):
-        copy = remote(ref, ref, send, recv, end)
-        relays.append(copy)
-
         @pl.when(middle)
         def _():
-            copy.start()
+            remote(ref, ref, send, recv, end).start()
 
     def along_z(n):
         here = parts[n](c, z, p)
-        for k in range(1, 3):
+        for k, to in enumerate(targets):
             copy = remote(
-                here, here, wa_send.at[n, k], wa_recv.at[n, z], (p, 2 * nearest(z, k) + c)
+                here, here, wa_send.at[n, 1 + k], wa_recv.at[n, z], (p, 2 * to + c)
             )
             copy.start()
             started.append(copy)
 
     def along_dp(n):
-        for k in range(1, 4):
-            zz = nearest(z, k)
+        for k in (1, 3, 2):
+            zz = visit(z, k)
             here = parts[n](c, zz, p)
             remote(here, here, wa_send.at[n, 0], wa_recv.at[n, zz], sibling).wait_recv()
-            if k > 1:
-                relay(here, wa_send.at[n, 1 + k], wa_recv.at[n, zz])
+            if k != 2:
+                relay(here, wa_send.at[n, 3 + k // 2], wa_recv.at[n, zz])
             for m in range(1, 4):
                 copy = remote(
                     here, here, wb_send.at[n, k, m], wb_recv.at[n, zz, p],
@@ -110,7 +112,7 @@
 
     def along_core(n):
         for k in range(1, 4):
-            zz = nearest(z, k)
+            zz = visit(z, k)
             for m in range(1, 4):
                 pp = lax.rem(p + m, 4)
                 there = parts[n](c, zz, pp)
@@ -128,9 +130,9 @@
     meansq = jnp.mean(x * x, axis=-1, keepdims=True)
     normed = x * lax.rsqrt(meansq + 1e-06) * ngain_ref[...][None, :]
     win[s] = jax.nn.gelu(normed).astype(jnp.bfloat16)
-    for k in range(1, 3):
+    for k, to in enumerate(targets):
         copy = remote(
-            win.at[s], win.at[s], act_send.at[k], act_recv.at[s], (p, 2 * nearest(z, k) + c)
+            win.at[s], win.at[s], act_send.at[1 + k], act_recv.at[s], (p, 2 * to + c)
         )
         copy.start()
         started.append(copy)
@@ -169,22 +171,33 @@
         bias8[j] = bias_row[:, j * width : (j + 1) * width]
         again8[j] = again_row[:, j * width : (j + 1) * width]
 
+    def hand_over(k):
+        b = 2 * visit(z, k) + c
+        return remote(win.at[b], win.at[b], act_send.at[3 + k], act_recv.at[b], sibling)
+
+    def take(k):
+        b = 2 * visit(z, k) + c
+        wait_block(b)
+        if k != 2:
+            relay(win.at[b], act_send.at[7 + k // 2], act_recv.at[b])
+        hand_over(k).start()
+
     def step(k):
-        zz = nearest(z, k)
-        if k > 0:
-            b = 2 * zz + c
-            wait_block(b)
-            copy = remote(
-                win.at[b], win.at[b], act_send.at[3 + k], act_recv.at[b], sibling
-            )
-            if k > 1:
-                relay(win.at[b], act_send.at[5 + k], act_recv.at[b])
-            copy.start()
-            started.append(copy)
         if k == 3:
+            @pl.when(jnp.logical_not(middle))
+            def _():
+                wait_block(2 * visit(z, 3) + c)
+                hand_over(3).start()
+
             along_dp(1)
-        wait_block(2 * zz + other)
-        convolve_pair(zz)
+        elif k > 0:
+            if k == 2:
+                @pl.when(middle)
+                def _():
+                    take(3)
+            take(k)
+        wait_block(2 * visit(z, k) + other)
+        convolve_pair(visit(z, k))
 
     def pooled(r, out):
         start = pl.multiple_of(r * block, 8) + EDGE
@@ -248,7 +261,7 @@
     kvbuf[s] = kv.astype(jnp.bfloat16)
     for k in range(1, 4):
         copy = remote(
-            kvbuf.at[s], kvbuf.at[s], kv_send.at[k], kv_recv.at[s], (p, 2 * nearest(z, k) + c)
+            kvbuf.at[s], kvbuf.at[s], kv_send.at[k], kv_recv.at[s], (p, 2 * visit(z, k) + c)
         )
         copy.start()
         started.append(copy)
@@ -267,14 +280,14 @@
         [query[:, h * HEAD_DIM : (h + 1) * HEAD_DIM] for h in range(heads)], axis=0
     )
     for k in range(1, 4):
-        b = 2 * nearest(z, k) + c
+        b = 2 * visit(z, k) + c
         remote(kvbuf.at[b], kvbuf.at[b], kv_send.at[0], kv_recv.at[b], sibling).wait_recv()
         copy = remote(kvbuf.at[b], kvbuf.at[b], kv_send.at[3 + k], kv_recv.at[b], sibling)
         copy.start()
         started.append(copy)
     along_core(1)
     for k in range(4):
-        b = 2 * nearest(z, k) + other
+        b = 2 * visit(z, k) + other
         remote(kvbuf.at[b], kvbuf.at[b], kv_send.at[0], kv_recv.at[b], sibling).wait_recv()
 
     keyvals = kvbuf[...].reshape(8 * half, kvbuf.shape[2])
@@ -308,11 +321,17 @@
 
     for copy in started:
         copy.wait_send()
+    for k in range(1, 4):
+        hand_over(k).wait_send()
 
     @pl.when(middle)
     def _():
-        for copy in relays:
-            copy.wait_send()
+        for n in range(2):
+            for m in range(3, 5):
+                here = parts[n](c, z, p)
+                remote(here, here, wa_send.at[n, m], wa_recv.at[n, z], end).wait_send()
+        for m in range(7, 9):
+            remote(win.at[s], win.at[s], act_send.at[m], act_recv.at[s], end).wait_send()
 
 
 def fused(
@@ -364,7 +383,7 @@
             dma((8,)), dma((8,)),
         ],
         compiler_params=pltpu.CompilerParams(
-            collective_id=0, has_side_effects=True, vmem_limit_bytes=60 * 1024 * 1024
+            collective_id=0, has_side_effects=True, vmem_limit_bytes=52 * 1024 * 1024
         ),
     )(
         features,

time: 88.4 us -> 97.6 us (1.10)
  Pallas kernels: 84.2 us -> 89.2 us
  local copies, waits for them, and re-layouts: 3.39 us -> 7.05 us
    pallas_call x1, Pallas kernels: 84.2 us -> 89.2 us  [fused(): pl.pallas_call(fused_kernel, out_shape=(jax.ShapeDtypeStruct((half, total...]
    unnamed x2 -> x16, local copies, waits for them, and re-layouts: 3.39 us -> 7.05 us
where the time goes in v6:
time: 97.6 us; the launch traced here: 96.9 us
  Pallas kernels  89.2 us (91%)
  local copies, waits for them, and re-layouts  7.05 us (7%)
    pallas_call x1, Pallas kernels, fused(): pl.pallas_call(fused_kernel, out_shape=(jax.ShapeDtypeStruct((half, total...  89.2 us
    unnamed x16, local copies, waits for them, and re-layouts  7.05 us

profile of v6, /device:TPU:1, one launch (start us, length us, event | category | flops | bytes accessed | tf_op | source)
XLA Modules:
  0.0 96.9 jit_solution(9144646903197363020)
XLA Ops:
  0.6 0.0 copy-start
  0.6 1.0 %copy-done = bf16[192,1024]{1,0:T(8,128)(2,1)S(1)} copy-done((bf16[192,1024]{1,0:T(8,128)(2,1)S(1)}, bf16[192,1024]{1,0:T(8,128)(2,1)}, u32[]{:S(2)}) %copy-start) | copy-done | bytes 393240
  1.6 0.0 copy-start.1
  1.6 1.0 %copy-done.1 = bf16[128,1536]{1,0:T(8,128)(2,1)S(1)} copy-done((bf16[128,1536]{1,0:T(8,128)(2,1)S(1)}, bf16[128,1536]{1,0:T(8,128)(2,1)}, u32[]{:S(2)}) %copy-start.1) | copy-done | bytes 393240
  2.6 0.0 copy-start.2
  2.6 0.9 copy-done.2
  3.5 0.0 copy-start.3
  3.5 0.7 copy-done.3
  4.2 0.0 copy-start.4
  4.2 0.7 copy-done.4
  4.9 0.0 copy-start.5
  4.9 0.7 copy-done.5
  5.6 0.0 copy-start.6
  5.6 0.7 copy-done.6
  6.3 89.2 %shard_map.104 = (bf16[96,1536]{1,0:T(8,128)(2,1)S(1)}, bf16[96,1536]{1,0:T(8,128)(2,1)S(1)}) custom-call(bf16[192,1408]{1,0:T(8,128)(2,1)} %feat_ref.1, f32[1408]{0:T(1024)S(1)} %copy-done.3, bf16[5,192,1408]{2,1,0:T(8,128)(2,1)} %bitcast.1, f32[1536]{0:T(1024)S(1)} %copy-done.4, f32[1536]{0:T(1024)S(1)} %copy-done.5, bf16[192,1024]{1,0:T(8,128)(2,1)S(1)} %copy-done, ...), custom_call_target="tpu_custom_call" | custom-call | tf_op jit(solution)/shard_map/pallas_call | solution.py:352
  95.4 0.7 copy.13
  96.2 0.7 copy.14
Async XLA Ops:
  0.6 1.0 %copy-start = (bf16[192,1024]{1,0:T(8,128)(2,1)S(1)}, bf16[192,1024]{1,0:T(8,128)(2,1)}, u32[]{:S(2)}) copy-start(bf16[192,1024]{1,0:T(8,128)(2,1)} %wq_ref.1) | copy-start | bytes 1179652
  1.6 1.0 %copy-start.1 = (bf16[128,1536]{1,0:T(8,128)(2,1)S(1)}, bf16[128,1536]{1,0:T(8,128)(2,1)}, u32[]{:S(2)}) copy-start(bf16[128,1536]{1,0:T(8,128)(2,1)} %wo_ref.1) | copy-start | bytes 1179652
  2.6 0.9 copy-start.2
  3.5 0.7 copy-start.3
  4.2 0.7 copy-start.4
  4.9 0.7 copy-start.5
  5.6 0.7 copy-start.6

commit v7 on v5

--- a/solution.py
+++ b/solution.py
@@ -128,15 +128,15 @@
     meansq = jnp.mean(x * x, axis=-1, keepdims=True)
     normed = x * lax.rsqrt(meansq + 1e-06) * ngain_ref[...][None, :]
     win[s] = jax.nn.gelu(normed).astype(jnp.bfloat16)
+    copy = remote(win.at[s], win.at[s], act_send.at[0], act_recv.at[s], sibling)
+    copy.start()
+    started.append(copy)
     for k in range(1, 3):
         copy = remote(
             win.at[s], win.at[s], act_send.at[k], act_recv.at[s], (p, 2 * nearest(z, k) + c)
         )
         copy.start()
         started.append(copy)
-    copy = remote(win.at[s], win.at[s], act_send.at[0], act_recv.at[s], sibling)
-    copy.start()
-    started.append(copy)
 
     acc0[...] = jnp.zeros_like(acc0)
     acc1[...] = jnp.zeros_like(acc1)
@@ -206,8 +206,8 @@
         copy.start()
         started.append(copy)
 
+    along_dp(0)
     step(0)
-    along_dp(0)
     step(1)
     along_z(1)
     step(2)

time: 88.4 us -> 88.4 us (level)
  no operation moved by 1% of the time
where the time goes in v7:
time: 88.4 us; the launch traced here: 88.2 us
  Pallas kernels  84.2 us (95%)
  local copies, waits for them, and re-layouts  3.39 us (4%)
    pallas_call x1, Pallas kernels, fused(): pl.pallas_call(fused_kernel, out_shape=(jax.ShapeDtypeStruct((half, total...  84.2 us
    unnamed x2, local copies, waits for them, and re-layouts  3.39 us

profile of v7, /device:TPU:1, one launch (start us, length us, event | category | flops | bytes accessed | tf_op | source)
XLA Modules:
  0.0 88.2 jit_solution(3879878218326819392)
XLA Ops:
  0.6 84.2 %shard_map.104 = (bf16[96,1536]{1,0:T(8,128)(2,1)}, bf16[96,1536]{1,0:T(8,128)(2,1)}) custom-call(bf16[192,1408]{1,0:T(8,128)(2,1)} %feat_ref.1, f32[1408]{0:T(1024)} %ngain_ref.1, bf16[5,192,1408]{2,1,0:T(8,128)(2,1)} %bitcast.1, f32[1536]{0:T(1024)} %bias_ref.1, f32[1536]{0:T(1024)} %again_ref.1, bf16[192,1024]{1,0:T(8,128)(2,1)} %wq_ref.1, ...), custom_call_target="tpu_custom_call" | custom-call | tf_op jit(solution)/shard_map/pallas_call | solution.py:333
  84.8 1.7 %copy.13 = bf16[96,1536]{1,0:T(8,128)(2,1)} copy(bf16[96,1536]{1,0:T(8,128)(2,1)} %get-tuple-element.4) | data formatting | bytes 589824
  86.5 1.7 %copy.14 = bf16[96,1536]{1,0:T(8,128)(2,1)} copy(bf16[96,1536]{1,0:T(8,128)(2,1)} %get-tuple-element.5) | data formatting | bytes 589824

commit v8 on v7

--- a/solution.py
+++ b/solution.py
@@ -181,8 +181,6 @@
                 relay(win.at[b], act_send.at[5 + k], act_recv.at[b])
             copy.start()
             started.append(copy)
-        if k == 3:
-            along_dp(1)
         wait_block(2 * zz + other)
         convolve_pair(zz)
 
@@ -220,6 +218,7 @@
     step(3)
     for k in range(5, 8):
         send_rows(k, k + upper * (7 - 2 * k))
+    along_dp(1)
     for k in range(1, 8):
         r = lax.rem(s + k, 8)
         remote(csend.at[r], cbuf.at[r], co_send.at[0], co_recv.at[r], sibling).wait_recv()

time: 88.4 us -> 90.5 us (1.024); the launches traced: 88.2 us -> 89 us
  no operation moved by 1% of the time
where the time goes in v8:
time: 90.5 us; the launch traced here: 89 us
  Pallas kernels  85 us (94%)
  local copies, waits for them, and re-layouts  3.39 us (4%)
    pallas_call x1, Pallas kernels, fused(): pl.pallas_call(fused_kernel, out_shape=(jax.ShapeDtypeStruct((half, total...  85 us
    unnamed x2, local copies, waits for them, and re-layouts  3.39 us

profile of v8, /device:TPU:1, one launch (start us, length us, event | category | flops | bytes accessed | tf_op | source)
XLA Modules:
  0.0 89.0 jit_solution(17301133925008477758)
XLA Ops:
  0.6 85.0 %shard_map.104 = (bf16[96,1536]{1,0:T(8,128)(2,1)}, bf16[96,1536]{1,0:T(8,128)(2,1)}) custom-call(bf16[192,1408]{1,0:T(8,128)(2,1)} %feat_ref.1, f32[1408]{0:T(1024)} %ngain_ref.1, bf16[5,192,1408]{2,1,0:T(8,128)(2,1)} %bitcast.1, f32[1536]{0:T(1024)} %bias_ref.1, f32[1536]{0:T(1024)} %again_ref.1, bf16[192,1024]{1,0:T(8,128)(2,1)} %wq_ref.1, ...), custom_call_target="tpu_custom_call" | custom-call | tf_op jit(solution)/shard_map/pallas_call | solution.py:332
  85.6 1.7 %copy.13 = bf16[96,1536]{1,0:T(8,128)(2,1)} copy(bf16[96,1536]{1,0:T(8,128)(2,1)} %get-tuple-element.4) | data formatting | bytes 589824
  87.3 1.7 %copy.14 = bf16[96,1536]{1,0:T(8,128)(2,1)} copy(bf16[96,1536]{1,0:T(8,128)(2,1)} %get-tuple-element.5) | data formatting | bytes 589824
